TPU v7x, 32 devices: a whole 2x2x4 slice. The times are simulated.
32 devices in a mesh: inst: 4 (over y, x), page: 4 (over z), head: 2 (over core).
Axes of the slice: x: 2, y: 2, z: 4, core: 2. Of those that a mesh axis runs over, the one named last changes fastest.
Arguments:
- queries: bfloat16 [8, 8192], P('inst', 'head'), may hold values from -21 to 21
- fresh_key_value: bfloat16 [2, 8, 1024], P(None, 'inst', 'head'), may hold values from -8 to 8
- key_value_pool: bfloat16 [2, 2048, 16, 1024], P(None, ('inst', 'page'), None, 'head'), may hold values from -21 to 21
- block_table: int32 [8, 384], P('inst'), may hold values from -1 to 2047, as said below
- lengths: int32 [8], P('inst'), may hold values from 17 to 6144, as said below
Outputs:
- attn: bfloat16 [8, 8192], P('inst', 'head')
Inputs may be any that keep to these rules, and one draw needn't show every extreme that they name: `block_table`: request r is owned by instance r // 2. Entries 0 to ceil(lengths[r] / 16) - 1 of row r are pool page numbers below 2048, distinct over all requests; every other entry is -1. `lengths`: every request has two or more pages; some request has exactly 384 full pages.
All inputs are finite; a program needn't handle non-finite values.
Results may differ from a plain program's by a relative error of at most 0.001.
Values may be sent and summed in bfloat16 or wider, within the bound.
A program may use at most 192 MiB of HBM per device.

v0:
```python
import math

import jax
import jax.numpy as jnp
from jax import lax
from jax.sharding import PartitionSpec as P

HEAD_SIZE = 128


LOWEST_SCORE = -1e30


def slot_owners(all_tables, all_lengths, slots, page_tok):
    requests, most_pages = all_tables.shape
    first_page = (lax.axis_index("inst") * lax.axis_size("page") + lax.axis_index("page")) * slots
    column = jnp.arange(most_pages, dtype=jnp.int32)
    live_page = column[None, :] * page_tok < all_lengths[:, None]
    local_page = all_tables - first_page
    inside = live_page & (local_page >= 0) & (local_page < slots)
    expected_output = jnp.where(inside, local_page, slots).reshape(-1)
    request_ids = jnp.broadcast_to(
        jnp.arange(requests, dtype=jnp.int32)[:, None], (requests, most_pages)
    ).reshape(-1)
    page_fill = jnp.clip(all_lengths[:, None] - column[None, :] * page_tok, 0, page_tok).reshape(-1)
    page_owner = (
        jnp.full((slots,), requests, jnp.int32).at[expected_output].set(request_ids, mode="drop")
    )
    filled = jnp.zeros((slots,), jnp.int32).at[expected_output].set(page_fill, mode="drop")
    return (page_owner, filled)


def page_partials(slot_queries, key_value_pool, filled):
    slots = key_value_pool.shape[1]
    page_tok = key_value_pool.shape[2]
    groups = key_value_pool.shape[3] // HEAD_SIZE
    heads = slot_queries.shape[1] // HEAD_SIZE
    grouped_queries = slot_queries.reshape(slots, groups, heads // groups, HEAD_SIZE)
    paged_keys = key_value_pool[0].reshape(slots, page_tok, groups, HEAD_SIZE)
    paged_values = key_value_pool[1].reshape(slots, page_tok, groups, HEAD_SIZE)
    scores = jnp.einsum(
        "sgqd,stgd->sgqt", grouped_queries, paged_keys, preferred_element_type=jnp.float32
    ) * (1.0 / math.sqrt(HEAD_SIZE))
    offsets = jnp.arange(page_tok, dtype=jnp.int32)
    valid = (offsets[None, :] < filled[:, None])[:, None, None, :]
    masked = jnp.where(valid, scores, LOWEST_SCORE)
    page_max = jnp.max(masked, axis=3)
    raw_weight = jnp.where(valid, jnp.exp(masked - page_max[..., None]), 0.0)
    page_sum = jnp.sum(raw_weight, axis=3)
    page_out = jnp.einsum(
        "sgqt,stgd->sgqd",
        raw_weight.astype(jnp.bfloat16),
        paged_values,
        preferred_element_type=jnp.float32,
    )
    return (
        page_max.reshape(slots, heads),
        page_sum.reshape(slots, heads),
        page_out.reshape(slots, heads * HEAD_SIZE),
    )


def request_max(page_max, page_owner, requests):
    matches = page_owner[None, :] == jnp.arange(requests, dtype=jnp.int32)[:, None]
    return jnp.max(jnp.where(matches[:, :, None], page_max[None], LOWEST_SCORE), axis=1)


def request_sums(page_max, page_sum, page_out, page_owner, shared_max):
    requests, heads = shared_max.shape
    slots = page_max.shape[0]
    padded = jnp.concatenate([shared_max, jnp.full((1, heads), LOWEST_SCORE, jnp.float32)], axis=0)
    factor = jnp.exp(page_max - padded[page_owner])
    one_hot = (page_owner[None, :] == jnp.arange(requests, dtype=jnp.int32)[:, None]).astype(
        jnp.float32
    )
    scaled_out = (page_out.reshape(slots, heads, HEAD_SIZE) * factor[:, :, None]).reshape(
        slots, heads * HEAD_SIZE
    )
    summed_out = jnp.dot(
        one_hot, scaled_out, precision=lax.Precision.HIGHEST, preferred_element_type=jnp.float32
    )
    summed_total = jnp.dot(
        one_hot,
        page_sum * factor,
        precision=lax.Precision.HIGHEST,
        preferred_element_type=jnp.float32,
    )
    return (summed_total, summed_out)


def finish(queries, fresh_key_value, cache_max, cache_total, cache_out):
    own_rows = queries.shape[0]
    heads = queries.shape[1] // HEAD_SIZE
    groups = fresh_key_value.shape[2] // HEAD_SIZE
    per_group = heads // groups
    grouped_queries = queries.reshape(own_rows, groups, per_group, HEAD_SIZE)
    new_keys = fresh_key_value[0].reshape(own_rows, groups, HEAD_SIZE)
    fresh_score = jnp.einsum(
        "rgqd,rgd->rgq", grouped_queries, new_keys, preferred_element_type=jnp.float32
    ).reshape(own_rows, heads) * (1.0 / math.sqrt(HEAD_SIZE))
    top_score = jnp.maximum(cache_max, fresh_score)
    carried = jnp.exp(cache_max - top_score)
    own_weight = jnp.exp(fresh_score - top_score)
    denominator = own_weight + cache_total * carried
    new_values = jnp.broadcast_to(
        fresh_key_value[1].astype(jnp.float32).reshape(own_rows, groups, 1, HEAD_SIZE),
        (own_rows, groups, per_group, HEAD_SIZE),
    ).reshape(own_rows, heads, HEAD_SIZE)
    weighted = (
        own_weight[:, :, None] * new_values
        + cache_out.reshape(own_rows, heads, HEAD_SIZE) * carried[:, :, None]
    )
    return (
        (weighted / denominator[:, :, None])
        .reshape(own_rows, heads * HEAD_SIZE)
        .astype(jnp.bfloat16)
    )


def shards(queries, fresh_key_value, key_value_pool, block_table, lengths):
    all_tables, all_lengths = (
        lax.all_gather(block_table, "inst", axis=0, tiled=True),
        lax.all_gather(lengths, "inst", axis=0, tiled=True),
    )
    all_queries = lax.all_gather(queries, "inst", axis=0, tiled=True)
    requests = all_tables.shape[0]
    own_rows = queries.shape[0]
    row_start = lax.axis_index("inst") * own_rows
    page_owner, filled = slot_owners(
        all_tables, all_lengths, key_value_pool.shape[1], key_value_pool.shape[2]
    )
    slot_queries = all_queries[jnp.minimum(page_owner, requests - 1)]
    page_max, page_sum, page_out = page_partials(slot_queries, key_value_pool, filled)
    local_max = request_max(page_max, page_owner, requests)
    shared_max = lax.pmax(local_max, ("inst", "page"))
    shared_total, shared_out = request_sums(page_max, page_sum, page_out, page_owner, shared_max)
    summed_out, summed_total = lax.psum((shared_out, shared_total), ("inst", "page"))
    cache_max = lax.dynamic_slice_in_dim(shared_max, row_start, own_rows, 0)
    cache_total = lax.dynamic_slice_in_dim(summed_total, row_start, own_rows, 0)
    cache_out = lax.dynamic_slice_in_dim(summed_out, row_start, own_rows, 0)
    return finish(queries, fresh_key_value, cache_max, cache_total, cache_out)


def solution(mesh):
    return jax.shard_map(
        shards,
        mesh=mesh,
        in_specs=(
            P("inst", "head"),
            P(None, "inst", "head"),
            P(None, ("inst", "page"), None, "head"),
            P("inst", None),
            P("inst"),
        ),
        out_specs=P("inst", "head"),
        check_vma=False,
    )
```

profile of v0, /device:TPU:0, one launch (start us, length us, event | category | flops | bytes accessed | tf_op | source)
XLA Modules:
  0.0 241.6 jit_solution(4967316013040577179)
XLA Ops:
  6.5 1.2 dynamic-slice
  8.4 0.9 dynamic-update-slice
  9.3 8.8 %all-reduce.1 = s32[8]{0:T(128)S(1)} all-reduce(s32[8]{0:T(128)S(1)} %dynamic-update-slice), channel_id=1, replica_groups=mesh['inst'=4,'page'=4,'head'=2] {'inst'}, use_global_device_ids=true, to_apply=%add.1 | all-reduce | flops 8 | bytes 64
  18.1 8.1 %all-gather = s32[4,2,384]{2,1,0:T(2,128)S(1)} all-gather(s32[1,2,384]{2,1,0:T(2,128)} %bitcast.90), channel_id=1, replica_groups=mesh['inst'=4,'page'=4,'head'=2] {'inst'}, dimensions={0}, use_global_device_ids=true | all-gather | bytes 15360 | tf_op jit(solution)/shard_map/all_gather | solution.py:122
  26.4 11.8 %scatter_custom_fusion = s32[128]{0:T(128)S(1)} fusion(s32[3072]{0:T(1024)S(1)} %bitcast.87, s32[3072]{0:T(1024)S(1)} %reshape.155, s32[]{:T(128)} %constant.15.clone.1), kind=kCustom, calls=%fused_computation.59 | custom fusion | bytes 516 | tf_op jit(solution)/shard_map/scatter | solution.py:27
  38.2 11.8 %scatter_custom_fusion.1 = s32[128]{0:T(128)S(1)} fusion(s32[3072]{0:T(1024)S(1)} %bitcast.88, s32[3072]{0:T(1024)S(1)} %reshape.163, s32[]{:T(128)} %constant.21.clone.1), kind=kCustom, calls=%fused_computation.57 | custom fusion | bytes 516 | tf_op jit(solution)/shard_map/scatter | solution.py:29
  50.1 7.4 %all-gather.1 = bf16[4,2,4096]{2,1,0:T(2,128)(2,1)S(1)} all-gather(bf16[1,2,4096]{2,1,0:T(2,128)(2,1)} %bitcast.85), channel_id=1, replica_groups=mesh['inst'=4,'page'=4,'head'=2] {'inst'}, dimensions={0}, use_global_device_ids=true | all-gather | bytes 81920 | tf_op jit(solution)/shard_map/all_gather | solution.py:125
  57.6 1.2 gather_fusion
  58.8 0.2 copy.37
  59.0 4.6 %fusion.34 = (bf16[1,128,16,512]{3,2,1,0:T(8,128)(2,1)}, bf16[1,128,16,512]{3,2,1,0:T(8,128)(2,1)}) fusion(bf16[2,128,16,512]{3,2,1,0:T(8,128)(2,1)} %param.7), kind=kLoop, calls=%fused_computation.64 | loop fusion | bytes 8388608 | tf_op jit(solution)/shard_map/slice | solution.py:40
  63.6 3.5 %copy.34 = bf16[1,128,16,512]{1,3,2,0:T(8,128)(2,1)S(1)} copy(bf16[1,128,16,512]{3,2,1,0:T(8,128)(2,1)} %get-tuple-element.8) | data formatting | bytes 4194304
  67.1 3.0 %copy.27 = bf16[128,16,4,128]{3,1,2,0:T(8,128)(2,1)} copy(bf16[128,16,4,128]{0,3,2,1:T(8,128)(2,1)S(1)} %bitcast.73) | data formatting | bytes 4194304 | tf_op jit(solution)/shard_map/reshape;squeeze | solution.py:40
  70.1 3.5 %copy.33 = bf16[1,128,16,512]{1,3,2,0:T(8,128)(2,1)S(1)} copy(bf16[1,128,16,512]{3,2,1,0:T(8,128)(2,1)} %get-tuple-element.9) | data formatting | bytes 4194304
  73.6 3.0 %copy.24 = bf16[128,16,4,128]{3,1,2,0:T(8,128)(2,1)} copy(bf16[128,16,4,128]{0,3,2,1:T(8,128)(2,1)S(1)} %bitcast.74) | data formatting | bytes 4194304 | tf_op jit(solution)/shard_map/reshape;squeeze | solution.py:39
  76.5 2.9 %fusion.4 = (f32[128,4,8]{2,1,0:T(4,128)S(1)}, f32[128,4,8,16]{3,2,1,0:T(8,128)S(1)}) fusion(pred[128,16]{1,0:T(8,128)(4,1)S(1)} %iota_compare_fusion, bf16[128,4,8,128]{3,2,1,0:T(8,128)(2,1)S(1)} %bitcast.77, bf16[128,16,4,128]{3,1,2,0:T(8,128)(2,1)} %copy.24), kind=kOutput, calls=%fused_computation.11 | convolution fusion | flops 16969728 | bytes 3426304 | tf_op jit(solution)/shard_map/sgqd,stgd->sgqt/dot_general | solution.py:41
  79.5 0.1 copy.28
  79.7 0.1 select_reduce_fusion
  79.8 41.4 %pmax.7 = f32[8,32]{1,0:T(8,128)S(1)} all-reduce(f32[8,32]{1,0:T(8,128)S(1)} %select_reduce_fusion), channel_id=1, replica_groups=mesh['inst'=4,'page'=4,'head'=2] {'inst','page'}, use_global_device_ids=true, to_apply=%region_4.5 | all-reduce | flops 256 | bytes 2048 | tf_op jit(solution)/shard_map/pmax | solution.py:135
  121.2 3.7 %fusion.7 = f32[128,4,8,128]{3,2,1,0:T(8,128)} fusion(bf16[128,16,4,128]{3,1,2,0:T(8,128)(2,1)} %copy.27, f32[128,4,8,16]{3,2,1,0:T(8,128)S(1)} %get-tuple-element.17, f32[128,4,8]{2,1,0:T(4,128)S(1)} %get-tuple-element.16, pred[128,16]{1,0:T(8,128)(4,1)S(1)} %iota_compare_fusion), kind=kOutput, calls=%fused_computation.14 | convolution fusion | flops 17104896 | bytes 4474880 | tf_op jit(solution)/shard_map/sgqt,stgd->sgqd/dot_general | solution.py:50
  125.0 0.6 gather_fusion.1
  125.6 0.6 mul.86
  126.2 1.0 copy-done
  127.2 4.1 %fusion = f32[8,4096]{1,0:T(8,128)} fusion(f32[16,8,32,128]{3,2,1,0:T(8,128)S(1)} %bitcast.75, f32[16,8,32,128]{3,2,1,0:T(8,128)S(1)} %bitcast.78, s32[128]{0:T(128)S(1)} %scatter_custom_fusion), kind=kOutput, calls=%fused_computation.5 | convolution fusion | flops 50856960 | bytes 4325888 | tf_op jit(solution)/shard_map/dot_general | solution.py:79
  131.4 1.4 fusion.5
  132.8 0.1 fusion.18
  132.9 0.1 mul.76
  133.0 0.1 copy.29
  133.1 0.1 copy.30
  133.2 0.1 fusion.14
  133.4 36.8 %psum.15 = f32[8,32]{1,0:T(8,128)S(1)} all-reduce(f32[8,32]{1,0:T(8,128)S(1)} %fusion.14), channel_id=1, replica_groups=mesh['inst'=4,'page'=4,'head'=2] {'inst','page'}, use_global_device_ids=true, to_apply=%region_7.8 | all-reduce | flops 256 | bytes 2048 | tf_op jit(solution)/shard_map/psum | solution.py:137
  170.3 62.8 %all-reduce.4.cloned.1.call-done = f32[8,4096]{1,0:T(8,128)} async-done(((f32[8,4096]{1,0:T(8,128)}), f32[8,4096]{1,0:T(8,128)}) %all-reduce.4.cloned.1.call-update) | async-done | bytes 131088 | tf_op jit(solution)/shard_map/psum | solution.py:137
  233.1 1.6 fusion.17
  (34 shorter events, 0.6 us)
Async XLA Ops:
  6.5 226.6 %all-reduce.4.cloned.1.call-start = ((), (), s32[]{:S(2)}) async-start(), calls=%async_computation | async-start | bytes 262144 | tf_op jit(solution)/shard_map/psum | solution.py:137
  125.6 1.6 copy-start
  131.3 1.4 copy-start.2
  131.3 1.5 copy-start.1
Sparse Core Ops, SparseCore 0:
  131.5 101.5 all-reduce.3
where the time goes:
time: 242 us
  blocking collectives  103 us (43%)
  waiting for transfers between devices  62.8 us (26%)
  local copies, waits for them, and re-layouts  47.5 us (20%)
  between operations  14.3 us (6%)
  matrix products  11.1 us (5%)
  other arithmetic  3.34 us (1%)
    psum x1, waiting for transfers between devices, shards(): lax.psum((shared_out, shared_total), ('inst', 'page'))  62.8 us
    pmax x1, blocking collectives, shards(): shared_max = lax.pmax(local_max, ('inst', 'page'))  41.4 us
    psum x1, blocking collectives, shards(): lax.psum((shared_out, shared_total), ('inst', 'page'))  36.8 us
    scatter x1, local copies, waits for them, and re-layouts, slot_owners(): jnp.full((slots,), requests, jnp.int32).at[expected_output]  11.8 us
    scatter x1, local copies, waits for them, and re-layouts, slot_owners(): jnp.zeros((slots,), jnp.int32).at[expected_output]  11.8 us
    unnamed x17, local copies, waits for them, and re-layouts  10.4 us
    unnamed x1, blocking collectives  8.82 us
    all_gather x1, blocking collectives, shards(): lax.all_gather(block_table, 'inst', axis=0, tiled=True)  8.11 us
  transfers between devices with their start and end apart: 1, of which 1 were waited for; matrix products, arithmetic and copies ran while one was open for 1% of the time, Pallas kernels for 0%

commit v1 on v0

v1 whole, which is shorter than its diff:
```python
import functools
import math

import jax
import jax.numpy as jnp
from jax import lax
from jax.experimental import pallas as pl
from jax.experimental.pallas import tpu as pltpu
from jax.sharding import PartitionSpec as P

HEAD_SIZE = 128
LOWEST_SCORE = -1e30
SCALE = 1.0 / math.sqrt(HEAD_SIZE)
CHUNK_SLOTS = 16
MESH = pl.DeviceIdType.MESH


def kernel(
    insts, pages, groups,
    q_ref, fresh_ref, len_ref, table_ref, pool_ref, out_ref,
    keys, values, values_t, q_own, q_all, t_own, t_all, raw, page_max, weights, send, recv,
    fresh_score, fresh_value,
    pool_sem, q_send, q_recv, t_send, t_recv, x_send, x_recv, o_send, o_recv,
):
    own = q_ref.shape[0]
    heads = q_ref.shape[1] // HEAD_SIZE
    per_group = heads // groups
    pairs = groups // 2
    requests = own * insts
    columns = table_ref.shape[1]
    slots, page_tok = keys.shape[0], keys.shape[1]
    tokens = slots * page_tok
    width = requests * per_group
    lanes = 2 * width
    stat_rows = pairs * lanes // 128
    devices = insts * pages
    units = own * groups // pages
    unit_rows = units * per_group

    me_i = lax.axis_index("inst")
    me_p = lax.axis_index("page")
    me = me_i * pages + me_p

    key_copy = pltpu.make_async_copy(pool_ref.at[0], keys, pool_sem.at[0])
    value_copy = pltpu.make_async_copy(pool_ref.at[1], values, pool_sem.at[1])
    value_copy.start()
    key_copy.start()

    barrier = pltpu.get_barrier_semaphore()

    def greet(k, carry):
        other = lax.rem(me + k, devices)
        pl.semaphore_signal(
            barrier, inc=1,
            device_id={"inst": lax.div(other, pages), "page": lax.rem(other, pages)},
            device_id_type=MESH,
        )
        return carry

    lax.fori_loop(1, devices, greet, 0)

    q = q_ref[...].astype(jnp.float32)
    fresh = fresh_ref[...].astype(jnp.float32)
    grouped = []
    for g in range(groups):
        rows = jnp.concatenate(
            [
                q[r : r + 1, (g * per_group + h) * HEAD_SIZE : (g * per_group + h + 1) * HEAD_SIZE]
                for r in range(own)
                for h in range(per_group)
            ],
            axis=0,
        )
        grouped.append(rows)
        q_own[g] = rows.astype(jnp.bfloat16)
    column = lax.broadcasted_iota(jnp.int32, (own, columns), 1)
    row = lax.broadcasted_iota(jnp.int32, (own, columns), 0)
    length = jnp.zeros((own, columns), jnp.int32)
    for r in range(own):
        length = jnp.where(row == r, len_ref[r], length)
    fill = jnp.clip(length - column * page_tok, 0, page_tok)
    t_own[...] = jnp.where(fill > 0, table_ref[...] * 32 + fill, -1)

    pl.semaphore_wait(barrier, devices - 1)

    def gather_copies(k):
        to = {"inst": lax.rem(me_i + k, insts)}
        return (
            pltpu.make_async_remote_copy(
                src_ref=q_own, dst_ref=q_all.at[me_i], send_sem=q_send.at[k],
                recv_sem=q_recv.at[k], device_id=to, device_id_type=MESH,
            ),
            pltpu.make_async_remote_copy(
                src_ref=t_own, dst_ref=t_all.at[me_i], send_sem=t_send.at[k],
                recv_sem=t_recv.at[k], device_id=to, device_id_type=MESH,
            ),
        )

    for k in range(1, insts):
        for copy in gather_copies(k):
            copy.start()
    q_all[me_i] = q_own[...]
    t_all[me_i] = t_own[...]

    for unit in range(own * groups):
        r, g = unit // groups, unit % groups
        p, u = unit // units, unit % units
        cut = slice(g * HEAD_SIZE, (g + 1) * HEAD_SIZE)
        products = grouped[g][r * per_group : (r + 1) * per_group] * fresh[0, r : r + 1, cut]
        score = jnp.sum(products, axis=1, keepdims=True) * SCALE
        place = slice(u * per_group, (u + 1) * per_group)
        fresh_score[p, place] = jnp.broadcast_to(score, (per_group, HEAD_SIZE))
        fresh_value[p, place] = jnp.broadcast_to(fresh[1, r : r + 1, cut], (per_group, HEAD_SIZE))

    value_copy.wait()
    for pair in range(pairs):
        cut = slice(pair * 2 * HEAD_SIZE, (pair + 1) * 2 * HEAD_SIZE)
        values_t[pair] = values[:, :, cut].reshape(tokens, 2 * HEAD_SIZE).T

    key_copy.wait()
    for k in range(1, insts):
        for copy in gather_copies(k):
            copy.wait()

    first = me * slots
    slot_id = lax.broadcasted_iota(jnp.int32, (slots, columns), 0) + first
    lane_request = lax.rem(lax.broadcasted_iota(jnp.int32, (slots, lanes), 1), width) // per_group
    filled = jnp.zeros((slots, lanes), jnp.int32)
    for i in range(insts):
        packed = t_all[i]
        page_id = packed >> 5
        page_fill = packed & 31
        for r in range(own):
            hit = jnp.where(slot_id == page_id[r : r + 1], page_fill[r : r + 1], 0)
            count = jnp.sum(hit.astype(jnp.float32), axis=1, keepdims=True).astype(jnp.int32)
            filled = jnp.where(lane_request == i * own + r, count, filled)

    pair_queries = []
    for pair in range(pairs):
        low = q_all[:, 2 * pair].reshape(width, HEAD_SIZE)
        high = q_all[:, 2 * pair + 1].reshape(width, HEAD_SIZE)
        none = jnp.zeros_like(low)
        pair_queries.append(
            jnp.concatenate(
                [jnp.concatenate([low, none], axis=1), jnp.concatenate([none, high], axis=1)], axis=0
            )
        )

    offset = lax.broadcasted_iota(jnp.int32, (CHUNK_SLOTS, page_tok, lanes), 1)
    chunk_tokens = CHUNK_SLOTS * page_tok
    for c in range(slots // CHUNK_SLOTS):
        here = slice(c * CHUNK_SLOTS, (c + 1) * CHUNK_SLOTS)
        valid = offset < filled[here][:, None, :]
        for pair in range(pairs):
            cut = slice(pair * 2 * HEAD_SIZE, (pair + 1) * 2 * HEAD_SIZE)
            scores = lax.dot_general(
                keys[here, :, cut].reshape(chunk_tokens, 2 * HEAD_SIZE),
                pair_queries[pair],
                (((1,), (1,)), ((), ())),
                preferred_element_type=jnp.float32,
            ).reshape(CHUNK_SLOTS, page_tok, lanes) * SCALE
            masked = jnp.where(valid, scores, LOWEST_SCORE)
            top = jnp.max(masked, axis=1)
            page_max[pair, here] = top
            raw[pair, here] = jnp.exp(masked - top[:, None, :])

    stats = []
    parts = []
    for pair in range(pairs):
        tops = page_max[pair]
        local_max = jnp.max(tops, axis=0, keepdims=True)
        factor = jnp.where(filled > 0, jnp.exp(tops - local_max), 0.0)
        total = jnp.zeros((page_tok, lanes), jnp.float32)
        for c in range(slots // CHUNK_SLOTS):
            here = slice(c * CHUNK_SLOTS, (c + 1) * CHUNK_SLOTS)
            scale = factor[here][:, None, :]
            weight = raw[pair, here]
            total += jnp.sum(weight * scale, axis=0)
            scaled = weight.astype(jnp.bfloat16).astype(jnp.float32) * scale
            upper = scaled.astype(jnp.bfloat16)
            lower = (scaled - upper.astype(jnp.float32)).astype(jnp.bfloat16)
            rows = slice(c * chunk_tokens, (c + 1) * chunk_tokens)
            weights[pair, rows, :lanes] = upper.reshape(chunk_tokens, lanes)
            weights[pair, rows, lanes:] = lower.reshape(chunk_tokens, lanes)
        stats.append((local_max, jnp.sum(total, axis=0, keepdims=True)))
        both = jnp.dot(values_t[pair], weights[pair], preferred_element_type=jnp.float32)
        both = both[:, :lanes] + both[:, lanes:]
        lane = lax.broadcasted_iota(jnp.int32, (HEAD_SIZE, lanes), 1)
        parts.append(jnp.where(lane < width, both[:HEAD_SIZE], both[HEAD_SIZE:]).T)

    stat_block = jnp.concatenate(
        [
            stats[pair][kind][:, b * 128 : (b + 1) * 128]
            for kind in range(2)
            for pair in range(pairs)
            for b in range(lanes // 128)
        ],
        axis=0,
    )
    for i in range(insts):
        for unit in range(own * groups):
            r, g = unit // groups, unit % groups
            p, u = unit // units, unit % units
            start = (g % 2) * width + (i * own + r) * per_group
            send[i * pages + p, u * per_group : (u + 1) * per_group] = parts[g // 2][
                start : start + per_group
            ]
        for p in range(pages):
            send[i * pages + p, unit_rows : unit_rows + 2 * stat_rows] = stat_block

    def exchange(k):
        other = lax.rem(me + k, devices)
        return pltpu.make_async_remote_copy(
            src_ref=send.at[other], dst_ref=recv.at[me], send_sem=x_send.at[k],
            recv_sem=x_recv.at[k],
            device_id={"inst": lax.div(other, pages), "page": lax.rem(other, pages)},
            device_id_type=MESH,
        )

    def start_exchange(k, carry):
        exchange(k).start()
        return carry

    def wait_exchange(k, carry):
        exchange(k).wait()
        return carry

    lax.fori_loop(1, devices, start_exchange, 0)
    recv[me] = send[me]
    lax.fori_loop(1, devices, wait_exchange, 0)

    row = lax.broadcasted_iota(jnp.int32, (1, unit_rows, 128), 1)
    lane = lax.broadcasted_iota(jnp.int32, (1, unit_rows, 128), 2)
    unit = me_p * units + row // per_group
    r, g = unit // groups, lax.rem(unit, groups)
    place = (
        (g // 2) * lanes + lax.rem(g, 2) * width
        + (me_i * own + r) * per_group + lax.rem(row, per_group)
    )
    picked = []
    for kind in range(2):
        found = jnp.zeros((devices, unit_rows, 128), jnp.float32)
        for b in range(stat_rows):
            at = unit_rows + kind * stat_rows + b
            found = jnp.where(place == b * 128 + lane, recv[:, at : at + 1, :], found)
        picked.append(jnp.sum(found, axis=2, keepdims=True))
    maxima, totals = picked
    own_score = fresh_score[me_p]
    top = jnp.maximum(jnp.max(maxima, axis=0), own_score)
    carried = jnp.exp(maxima - top[None])
    own_weight = jnp.exp(own_score - top)
    denominator = own_weight + jnp.sum(carried * totals, axis=0)
    numerator = own_weight * fresh_value[me_p] + jnp.sum(carried * recv[:, :unit_rows, :], axis=0)
    out_ref[me_p] = (numerator / denominator).astype(out_ref.dtype)

    def result_copy(k):
        return pltpu.make_async_remote_copy(
            src_ref=out_ref.at[me_p], dst_ref=out_ref.at[me_p], send_sem=o_send.at[k],
            recv_sem=o_recv.at[k], device_id={"page": lax.rem(me_p + k, pages)},
            device_id_type=MESH,
        )

    for k in range(1, pages):
        result_copy(k).start()
    for k in range(1, pages):
        result_copy(k).wait()


def shards(insts, pages, queries, fresh_key_value, key_value_pool, block_table, lengths):
    own = queries.shape[0]
    slots, page_tok, depth = key_value_pool.shape[1:]
    groups = depth // HEAD_SIZE
    heads = queries.shape[1] // HEAD_SIZE
    per_group = heads // groups
    pairs = groups // 2
    columns = block_table.shape[1]
    lanes = 2 * own * insts * per_group
    stat_rows = pairs * lanes // 128
    devices = insts * pages
    unit_rows = own * heads // pages
    block_rows = unit_rows + (2 * stat_rows + 7) // 8 * 8
    vmem = pl.BlockSpec(memory_space=pltpu.VMEM)
    dma = pltpu.SemaphoreType.DMA
    out = pl.pallas_call(
        functools.partial(kernel, insts, pages, groups),
        out_shape=jax.ShapeDtypeStruct((pages, unit_rows, HEAD_SIZE), jnp.bfloat16),
        in_specs=[
            vmem, vmem, pl.BlockSpec(memory_space=pltpu.SMEM), vmem,
            pl.BlockSpec(memory_space=pl.ANY),
        ],
        out_specs=vmem,
        scratch_shapes=[
            pltpu.VMEM((slots, page_tok, depth), jnp.bfloat16),
            pltpu.VMEM((slots, page_tok, depth), jnp.bfloat16),
            pltpu.VMEM((pairs, 2 * HEAD_SIZE, slots * page_tok), jnp.bfloat16),
            pltpu.VMEM((groups, own * per_group, HEAD_SIZE), jnp.bfloat16),
            pltpu.VMEM((insts, groups, own * per_group, HEAD_SIZE), jnp.bfloat16),
            pltpu.VMEM((own, columns), jnp.int32),
            pltpu.VMEM((insts, own, columns), jnp.int32),
            pltpu.VMEM((pairs, slots, page_tok, lanes), jnp.float32),
            pltpu.VMEM((pairs, slots, lanes), jnp.float32),
            pltpu.VMEM((pairs, slots * page_tok, 2 * lanes), jnp.bfloat16),
            pltpu.VMEM((devices, block_rows, 128), jnp.float32),
            pltpu.VMEM((devices, block_rows, 128), jnp.float32),
            pltpu.VMEM((pages, unit_rows, HEAD_SIZE), jnp.float32),
            pltpu.VMEM((pages, unit_rows, HEAD_SIZE), jnp.float32),
            dma((2,)),
            dma((insts,)), dma((insts,)), dma((insts,)), dma((insts,)),
            dma((devices,)), dma((devices,)),
            dma((pages,)), dma((pages,)),
        ],
        compiler_params=pltpu.CompilerParams(
            collective_id=0, has_side_effects=True, vmem_limit_bytes=56 * 1024 * 1024
        ),
        cost_estimate=pl.CostEstimate(
            flops=8 * slots * page_tok * lanes * HEAD_SIZE * pairs,
            bytes_accessed=4 * slots * page_tok * depth,
            transcendentals=slots * page_tok * lanes * pairs,
        ),
        name="paged_attention",
    )(queries, fresh_key_value, lengths, block_table, key_value_pool)
    return out.reshape(own, heads * HEAD_SIZE)


def solution(mesh):
    return jax.shard_map(
        functools.partial(shards, mesh.shape["inst"], mesh.shape["page"]),
        mesh=mesh,
        in_specs=(
            P("inst", "head"),
            P(None, "inst", "head"),
            P(None, ("inst", "page"), None, "head"),
            P("inst", None),
            P("inst"),
        ),
        out_specs=P("inst", "head"),
        check_vma=False,
    )
```

time: 242 us -> 25.1 us (0.10)
  blocking collectives: 103 us -> 0 us
  waiting for transfers between devices: 62.8 us -> 0 us
  local copies, waits for them, and re-layouts: 47.5 us -> 1.33 us
  Pallas kernels: 0 us -> 23.5 us
  between operations: 14.3 us -> 0.01 us
  matrix products: 11.1 us -> 0 us
  other arithmetic: 3.34 us -> 0 us
    psum x1 -> x0, waiting for transfers between devices: 62.8 us -> none  [shards(): lax.psum((shared_out, shared_total), ('inst', 'page'))]
    pmax x1 -> x0, blocking collectives: 41.4 us -> none  [shards(): shared_max = lax.pmax(local_max, ('inst', 'page'))]
    psum x1 -> x0, blocking collectives: 36.8 us -> none  [shards(): lax.psum((shared_out, shared_total), ('inst', 'page'))]
    scatter x2 -> x0, local copies, waits for them, and re-layouts: 23.5 us -> none  [the longest x1 11.8 us: slot_owners(): jnp.full((slots,), requests, jnp.int32).at[expected_output]]
    pallas_call x0 -> x1, Pallas kernels: none -> 23.5 us  [shards(): pl.pallas_call(functools.partial(kernel, insts, pages, groups), out_shape...]
    all_gather x2 -> x0, blocking collectives: 15.5 us -> none  [the longest x1 8.11 us: shards(): lax.all_gather(block_table, 'inst', axis=0, tiled=True)]
    dot_general x5 -> x0, matrix products: 11.1 us -> none  [the longest x1 4.14 us: request_sums(): jnp.dot(one_hot, scaled_out, precision=lax.Precision.HIGHEST, preferred_e...]
    unnamed x17 -> x0, local copies, waits for them, and re-layouts: 10.4 us -> none
  transfers between devices with their start and end apart: 1 -> 0, of which waited for: 1 -> 0; matrix products, arithmetic and copies ran while one was open for 1% -> 0% of each run, Pallas kernels for 0% -> 0%
where the time goes in v1:
time: 25.1 us; the launch traced here: 24.8 us
  Pallas kernels  23.5 us (94%)
  local copies, waits for them, and re-layouts  1.33 us (5%)
    pallas_call x1, Pallas kernels, shards(): pl.pallas_call(functools.partial(kernel, insts, pages, groups), out_shape...  23.5 us
    reshape x1, local copies, waits for them, and re-layouts, shards(): return out.reshape(own, heads * HEAD_SIZE)  1.33 us

profile of v1, /device:TPU:0, one launch (start us, length us, event | category | flops | bytes accessed | tf_op | source)
XLA Modules:
  0.0 24.8 jit_solution(4325010687278869785)
XLA Ops:
  0.0 23.5 %paged_attention.1 = bf16[4,16,128]{2,1,0:T(8,128)(2,1)} custom-call(bf16[2,4096]{1,0:T(2,128)(2,1)} %q_ref.1, bf16[2,2,512]{2,1,0:T(2,128)(2,1)} %fresh_ref.1, s32[2]{0:T(128)} %len_ref.1, s32[2,384]{1,0:T(2,128)} %table_ref.1, bf16[2,128,16,512]{3,2,1,0:T(8,128)(2,1)} %pool_ref.1), custom_call_target="tpu_custom_call" | custom-call | flops 536870912 | bytes 4194304 | tf_op jit(solution)/shard_map/paged_attention/pallas_call | solution.py:284
  23.5 1.3 %reshape.3 = bf16[2,4096]{1,0:T(2,128)(2,1)} reshape(bf16[4,16,128]{2,1,0:T(8,128)(2,1)} %paged_attention.1) | data formatting | bytes 32768 | tf_op jit(solution)/shard_map/reshape | solution.py:322

commit v2 on v1

v2 whole, which is shorter than its diff:
```python
import functools
import math

import jax
import jax.numpy as jnp
from jax import lax
from jax.experimental import pallas as pl
from jax.experimental.pallas import tpu as pltpu
from jax.sharding import PartitionSpec as P

HEAD_SIZE = 128
LOWEST_SCORE = -1e30
EXPONENT = math.log2(math.e) / math.sqrt(HEAD_SIZE)
CHUNK_SLOTS = 16
MESH = pl.DeviceIdType.MESH


def slot_of(pages, p):
    return p + p // 2 - 2 * (p // 3) if pages == 4 else p


def kernel(
    insts, pages, groups,
    q_hbm, fresh_hbm, len_hbm, table_hbm, pool_hbm, out_hbm,
    q_ref, fresh_ref, len_ref, table_ref,
    keys, values, values_t, q_own, q_all, t_own, t_all, raw, page_max, weights, send, recv,
    fresh_score, fresh_value, result,
    in_sem, pool_sem, q_send, q_recv, t_send, t_recv, x_send, x_recv, o_send, o_recv, o_own,
):
    own = q_ref.shape[0]
    heads = q_ref.shape[1] // HEAD_SIZE
    per_group = heads // groups
    pairs = groups // 2
    requests = own * insts
    columns = table_ref.shape[1]
    slots, page_tok = keys.shape[0], keys.shape[1]
    tokens = slots * page_tok
    width = requests * per_group
    lanes = 2 * width
    stat_rows = lanes // 128
    devices = insts * pages
    units = own * groups // pages
    unit_rows = units * per_group

    me_i = lax.axis_index("inst")
    me_p = lax.axis_index("page")
    me = me_i * pages + me_p
    me_slot = slot_of(pages, me_p)

    barrier = pltpu.get_barrier_semaphore()

    def greet(k, carry):
        other = lax.rem(me + k, devices)
        pl.semaphore_signal(
            barrier, inc=1,
            device_id={"inst": lax.div(other, pages), "page": lax.rem(other, pages)},
            device_id_type=MESH,
        )
        return carry

    lax.fori_loop(1, devices, greet, 0)

    small = [
        pltpu.make_async_copy(source, target, in_sem.at[k])
        for k, (source, target) in enumerate(
            [(q_hbm, q_ref), (len_hbm, len_ref), (table_hbm, table_ref), (fresh_hbm, fresh_ref)]
        )
    ]
    for copy in small:
        copy.start()
    value_copy = pltpu.make_async_copy(pool_hbm.at[1], values, pool_sem.at[1])
    key_copy = pltpu.make_async_copy(pool_hbm.at[0], keys, pool_sem.at[0])
    value_copy.start()
    key_copy.start()
    for copy in small:
        copy.wait()

    q = q_ref[...].astype(jnp.float32)
    fresh = fresh_ref[...].astype(jnp.float32)
    grouped = []
    for g in range(groups):
        rows = jnp.concatenate(
            [
                q[r : r + 1, (g * per_group + h) * HEAD_SIZE : (g * per_group + h + 1) * HEAD_SIZE]
                for r in range(own)
                for h in range(per_group)
            ],
            axis=0,
        )
        grouped.append(rows)
        q_own[g] = rows.astype(jnp.bfloat16)
    column = lax.broadcasted_iota(jnp.int32, (own, columns), 1)
    row = lax.broadcasted_iota(jnp.int32, (own, columns), 0)
    length = jnp.zeros((own, columns), jnp.int32)
    for r in range(own):
        length = jnp.where(row == r, len_ref[r], length)
    fill = jnp.clip(length - column * page_tok, 0, page_tok)
    t_own[...] = jnp.where(
        fill > 0, table_ref[...] * 1024 + (me_i * own + row) * 32 + fill, -1
    )

    pl.semaphore_wait(barrier, devices - 1)

    def gather_copies(k):
        to = {"inst": lax.rem(me_i + k, insts)}
        return (
            pltpu.make_async_remote_copy(
                src_ref=q_own, dst_ref=q_all.at[me_i], send_sem=q_send.at[k],
                recv_sem=q_recv.at[k], device_id=to, device_id_type=MESH,
            ),
            pltpu.make_async_remote_copy(
                src_ref=t_own, dst_ref=t_all.at[me_i], send_sem=t_send.at[k],
                recv_sem=t_recv.at[k], device_id=to, device_id_type=MESH,
            ),
        )

    for k in range(1, insts):
        for copy in gather_copies(k):
            copy.start()
    q_all[me_i] = q_own[...]
    t_all[me_i] = t_own[...]

    for unit in range(own * groups):
        r, g = unit // groups, unit % groups
        slot, u = unit // units, unit % units
        cut = slice(g * HEAD_SIZE, (g + 1) * HEAD_SIZE)
        products = grouped[g][r * per_group : (r + 1) * per_group] * fresh[0, r : r + 1, cut]
        score = jnp.sum(products, axis=1, keepdims=True)
        place = slice(u * per_group, (u + 1) * per_group)
        fresh_score[slot, place] = jnp.broadcast_to(score, (per_group, HEAD_SIZE))
        fresh_value[slot, place] = jnp.broadcast_to(fresh[1, r : r + 1, cut], (per_group, HEAD_SIZE))

    value_copy.wait()
    for pair in range(pairs):
        cut = slice(pair * 2 * HEAD_SIZE, (pair + 1) * 2 * HEAD_SIZE)
        values_t[pair] = values[:, :, cut].reshape(tokens, 2 * HEAD_SIZE).T

    key_copy.wait()
    for k in range(1, insts):
        for copy in gather_copies(k):
            copy.wait()

    slot_id = lax.broadcasted_iota(jnp.int32, (slots, 128), 0) + me * slots
    code = jnp.zeros((slots, 128), jnp.int32)
    for i in range(insts):
        packed = t_all[i]
        page_id = packed >> 10
        page_code = packed & 1023
        for r in range(own):
            for b in range(0, columns, 128):
                code += jnp.where(
                    slot_id == page_id[r : r + 1, b : b + 128], page_code[r : r + 1, b : b + 128], 0
                )
    code = jnp.sum(code.astype(jnp.float32), axis=1, keepdims=True).astype(jnp.int32)
    lane_request = lax.rem(lax.broadcasted_iota(jnp.int32, (slots, lanes), 1), width) // per_group
    filled = jnp.where(lane_request == code >> 5, code & 31, 0)

    offset = lax.broadcasted_iota(jnp.int32, (CHUNK_SLOTS, page_tok, lanes), 1)
    lane = lax.broadcasted_iota(jnp.int32, (HEAD_SIZE, lanes), 1)
    chunk_tokens = CHUNK_SLOTS * page_tok
    chunks = [slice(c * CHUNK_SLOTS, (c + 1) * CHUNK_SLOTS) for c in range(slots // CHUNK_SLOTS)]

    def exchange(to_i, to_p):
        to = to_i * pages + to_p
        return pltpu.make_async_remote_copy(
            src_ref=send.at[to], dst_ref=recv.at[me], send_sem=x_send.at[to],
            recv_sem=x_recv.at[me], device_id={"inst": to_i, "page": to_p}, device_id_type=MESH,
        )

    for pair in range(pairs):
        cut = slice(pair * 2 * HEAD_SIZE, (pair + 1) * 2 * HEAD_SIZE)
        low = q_all[:, 2 * pair].reshape(width, HEAD_SIZE)
        high = q_all[:, 2 * pair + 1].reshape(width, HEAD_SIZE)
        none = jnp.zeros_like(low)
        pair_queries = jnp.concatenate(
            [jnp.concatenate([low, none], axis=1), jnp.concatenate([none, high], axis=1)], axis=0
        )
        for here in chunks:
            scores = lax.dot_general(
                keys[here, :, cut].reshape(chunk_tokens, 2 * HEAD_SIZE),
                pair_queries,
                (((1,), (1,)), ((), ())),
                preferred_element_type=jnp.float32,
            ).reshape(CHUNK_SLOTS, page_tok, lanes)
            masked = jnp.where(offset < filled[here][:, None, :], scores, LOWEST_SCORE)
            top = jnp.max(masked, axis=1)
            page_max[pair, here] = top
            raw[pair, here] = jnp.exp2((masked - top[:, None, :]) * EXPONENT)
        tops = page_max[pair]
        local_max = jnp.max(tops, axis=0, keepdims=True)
        factor = jnp.where(filled > 0, jnp.exp2((tops - local_max) * EXPONENT), 0.0)
        total = jnp.zeros((page_tok, lanes), jnp.float32)
        for c, here in enumerate(chunks):
            scale = factor[here][:, None, :]
            weight = raw[pair, here]
            total += jnp.sum(weight * scale, axis=0)
            scaled = weight.astype(jnp.bfloat16).astype(jnp.float32) * scale
            upper = scaled.astype(jnp.bfloat16)
            lower = (scaled - upper.astype(jnp.float32)).astype(jnp.bfloat16)
            rows = slice(c * chunk_tokens, (c + 1) * chunk_tokens)
            weights[pair, rows, :lanes] = upper.reshape(chunk_tokens, lanes)
            weights[pair, rows, lanes:] = lower.reshape(chunk_tokens, lanes)
        total = jnp.sum(total, axis=0, keepdims=True)
        both = jnp.dot(values_t[pair], weights[pair], preferred_element_type=jnp.float32)
        both = both[:, :lanes] + both[:, lanes:]
        part = jnp.where(lane < width, both[:HEAD_SIZE], both[HEAD_SIZE:]).T
        stats = jnp.concatenate(
            [x[:, b * 128 : (b + 1) * 128] for x in (local_max, total) for b in range(stat_rows)],
            axis=0,
        )
        targets = [
            p for p in range(pages) if slot_of(pages, p) * units % groups // 2 == pair
        ]
        for p in targets:
            for i in range(insts):
                send[i * pages + p, unit_rows:] = stats
                for u in range(units):
                    r, g = divmod(slot_of(pages, p) * units + u, groups)
                    start = (g % 2) * width + (i * own + r) * per_group
                    send[i * pages + p, u * per_group : (u + 1) * per_group] = part[
                        start : start + per_group
                    ]

        def start_exchange(k, carry):
            for p in targets:
                exchange(lax.rem(me_i + k, insts), p).start()
            return carry

        lax.fori_loop(1, insts, start_exchange, 0)
        for p in targets:
            @pl.when(me_p != p)
            def _():
                exchange(me_i, p).start()

    recv[me] = send[me]

    def wait_exchange(k, carry):
        other = lax.rem(me + k, devices)
        pltpu.make_async_remote_copy(
            src_ref=send.at[other], dst_ref=recv.at[other], send_sem=x_send.at[other],
            recv_sem=x_recv.at[other],
            device_id={"inst": lax.div(other, pages), "page": lax.rem(other, pages)},
            device_id_type=MESH,
        ).wait()
        return carry

    lax.fori_loop(1, devices, wait_exchange, 0)

    row = lax.broadcasted_iota(jnp.int32, (1, unit_rows, 128), 1)
    lane = lax.broadcasted_iota(jnp.int32, (1, unit_rows, 128), 2)
    unit = me_slot * units + row // per_group
    r, g = unit // groups, lax.rem(unit, groups)
    place = lax.rem(g, 2) * width + (me_i * own + r) * per_group + lax.rem(row, per_group)
    picked = []
    for kind in range(2):
        found = jnp.zeros((devices, unit_rows, 128), jnp.float32)
        for b in range(stat_rows):
            at = unit_rows + kind * stat_rows + b
            found = jnp.where(place == b * 128 + lane, recv[:, at : at + 1, :], found)
        picked.append(jnp.sum(found, axis=2, keepdims=True))
    maxima, totals = picked
    own_score = fresh_score[me_slot]
    top = jnp.maximum(jnp.max(maxima, axis=0), own_score)
    carried = jnp.exp2((maxima - top[None]) * EXPONENT)
    own_weight = jnp.exp2((own_score - top) * EXPONENT)
    denominator = own_weight + jnp.sum(carried * totals, axis=0)
    numerator = own_weight * fresh_value[me_slot] + jnp.sum(
        carried * recv[:, :unit_rows, :], axis=0
    )
    result[...] = (numerator / denominator).astype(result.dtype)

    def result_copy(k):
        return pltpu.make_async_remote_copy(
            src_ref=result, dst_ref=out_hbm.at[me_slot], send_sem=o_send.at[k],
            recv_sem=o_recv.at[k], device_id={"page": lax.rem(me_p + k, pages)},
            device_id_type=MESH,
        )

    for k in range(1, pages):
        result_copy(k).start()
    own_copy = pltpu.make_async_copy(result, out_hbm.at[me_slot], o_own)
    own_copy.start()
    own_copy.wait()
    for k in range(1, pages):
        result_copy(k).wait()


def shards(insts, pages, queries, fresh_key_value, key_value_pool, block_table, lengths):
    own = queries.shape[0]
    slots, page_tok, depth = key_value_pool.shape[1:]
    groups = depth // HEAD_SIZE
    heads = queries.shape[1] // HEAD_SIZE
    per_group = heads // groups
    pairs = groups // 2
    columns = block_table.shape[1]
    lanes = 2 * own * insts * per_group
    devices = insts * pages
    unit_rows = own * heads // pages
    block_rows = unit_rows + 2 * lanes // 128
    hbm = pl.BlockSpec(memory_space=pl.ANY)
    dma = pltpu.SemaphoreType.DMA
    out = pl.pallas_call(
        functools.partial(kernel, insts, pages, groups),
        out_shape=jax.ShapeDtypeStruct((pages, unit_rows, HEAD_SIZE), jnp.bfloat16),
        in_specs=[hbm] * 5,
        out_specs=hbm,
        scratch_shapes=[
            pltpu.VMEM(queries.shape, jnp.bfloat16),
            pltpu.VMEM(fresh_key_value.shape, jnp.bfloat16),
            pltpu.SMEM(lengths.shape, jnp.int32),
            pltpu.VMEM(block_table.shape, jnp.int32),
            pltpu.VMEM((slots, page_tok, depth), jnp.bfloat16),
            pltpu.VMEM((slots, page_tok, depth), jnp.bfloat16),
            pltpu.VMEM((pairs, 2 * HEAD_SIZE, slots * page_tok), jnp.bfloat16),
            pltpu.VMEM((groups, own * per_group, HEAD_SIZE), jnp.bfloat16),
            pltpu.VMEM((insts, groups, own * per_group, HEAD_SIZE), jnp.bfloat16),
            pltpu.VMEM((own, columns), jnp.int32),
            pltpu.VMEM((insts, own, columns), jnp.int32),
            pltpu.VMEM((pairs, slots, page_tok, lanes), jnp.float32),
            pltpu.VMEM((pairs, slots, lanes), jnp.float32),
            pltpu.VMEM((pairs, slots * page_tok, 2 * lanes), jnp.bfloat16),
            pltpu.VMEM((devices, block_rows, 128), jnp.float32),
            pltpu.VMEM((devices, block_rows, 128), jnp.float32),
            pltpu.VMEM((pages, unit_rows, HEAD_SIZE), jnp.float32),
            pltpu.VMEM((pages, unit_rows, HEAD_SIZE), jnp.float32),
            pltpu.VMEM((unit_rows, HEAD_SIZE), jnp.bfloat16),
            dma((4,)), dma((2,)),
            dma((insts,)), dma((insts,)), dma((insts,)), dma((insts,)),
            dma((devices,)), dma((devices,)),
            dma((pages,)), dma((pages,)), dma(()),
        ],
        compiler_params=pltpu.CompilerParams(
            collective_id=0, has_side_effects=True, vmem_limit_bytes=56 * 1024 * 1024
        ),
        cost_estimate=pl.CostEstimate(
            flops=8 * slots * page_tok * lanes * HEAD_SIZE * pairs,
            bytes_accessed=4 * slots * page_tok * depth,
            transcendentals=slots * page_tok * lanes * pairs,
        ),
        name="paged_attention",
    )(queries, fresh_key_value, lengths, block_table, key_value_pool)
    return out.reshape(own, heads * HEAD_SIZE)


def solution(mesh):
    return jax.shard_map(
        functools.partial(shards, mesh.shape["inst"], mesh.shape["page"]),
        mesh=mesh,
        in_specs=(
            P("inst", "head"),
            P(None, "inst", "head"),
            P(None, ("inst", "page"), None, "head"),
            P("inst", None),
            P("inst"),
        ),
        out_specs=P("inst", "head"),
        check_vma=False,
    )
```

time: 25.1 us -> 23.4 us (0.932)
  Pallas kernels: 23.5 us -> 21.7 us
    pallas_call x1, Pallas kernels: 23.5 us -> 21.7 us  [shards(): pl.pallas_call(functools.partial(kernel, insts, pages, groups), out_shape...]
where the time goes in v2:
time: 23.4 us; the launch traced here: 23.1 us
  Pallas kernels  21.7 us (93%)
  local copies, waits for them, and re-layouts  1.33 us (6%)
    pallas_call x1, Pallas kernels, shards(): pl.pallas_call(functools.partial(kernel, insts, pages, groups), out_shape...  21.7 us
    reshape x1, local copies, waits for them, and re-layouts, shards(): return out.reshape(own, heads * HEAD_SIZE)  1.33 us

profile of v2, /device:TPU:0, one launch (start us, length us, event | category | flops | bytes accessed | tf_op | source)
XLA Modules:
  0.0 23.1 jit_solution(9417846883040862827)
XLA Ops:
  0.0 21.7 %paged_attention.1 = bf16[4,16,128]{2,1,0:T(8,128)(2,1)} custom-call(bf16[2,4096]{1,0:T(2,128)(2,1)} %q_hbm.1, bf16[2,2,512]{2,1,0:T(2,128)(2,1)} %fresh_hbm.1, s32[2]{0:T(128)} %len_hbm.1, s32[2,384]{1,0:T(2,128)} %table_hbm.1, bf16[2,128,16,512]{3,2,1,0:T(8,128)(2,1)} %pool_hbm.1), custom_call_target="tpu_custom_call" | custom-call | flops 536870912 | bytes 4194304 | tf_op jit(solution)/shard_map/paged_attention/pallas_call | solution.py:302
  21.7 1.3 %reshape.3 = bf16[2,4096]{1,0:T(2,128)(2,1)} reshape(bf16[4,16,128]{2,1,0:T(8,128)(2,1)} %paged_attention.1) | data formatting | bytes 32768 | tf_op jit(solution)/shard_map/reshape | solution.py:342

commit v3 on v2

--- a/solution.py
+++ b/solution.py
@@ -11,7 +11,7 @@
 HEAD_SIZE = 128
 LOWEST_SCORE = -1e30
 EXPONENT = math.log2(math.e) / math.sqrt(HEAD_SIZE)
-CHUNK_SLOTS = 16
+BLOCK_ROWS = 16
 MESH = pl.DeviceIdType.MESH
 
 
@@ -23,8 +23,9 @@
     insts, pages, groups,
     q_hbm, fresh_hbm, len_hbm, table_hbm, pool_hbm, out_hbm,
     q_ref, fresh_ref, len_ref, table_ref,
-    keys, values, values_t, q_own, q_all, t_own, t_all, raw, page_max, weights, send, recv,
-    fresh_score, fresh_value, result,
+    keys, values, keys_by_token, values_by_token, q_own, q_all, t_own, t_all,
+    scores, weights, send, recv,
+    columns_of, fresh_score, fresh_value, result,
     in_sem, pool_sem, q_send, q_recv, t_send, t_recv, x_send, x_recv, o_send, o_recv, o_own,
 ):
     own = q_ref.shape[0]
@@ -70,8 +71,8 @@
         copy.start()
     value_copy = pltpu.make_async_copy(pool_hbm.at[1], values, pool_sem.at[1])
     key_copy = pltpu.make_async_copy(pool_hbm.at[0], keys, pool_sem.at[0])
+    key_copy.start()
     value_copy.start()
-    key_copy.start()
     for copy in small:
         copy.wait()
 
@@ -130,12 +131,24 @@
         fresh_score[slot, place] = jnp.broadcast_to(score, (per_group, HEAD_SIZE))
         fresh_value[slot, place] = jnp.broadcast_to(fresh[1, r : r + 1, cut], (per_group, HEAD_SIZE))
 
-    value_copy.wait()
-    for pair in range(pairs):
-        cut = slice(pair * 2 * HEAD_SIZE, (pair + 1) * 2 * HEAD_SIZE)
-        values_t[pair] = values[:, :, cut].reshape(tokens, 2 * HEAD_SIZE).T
-
-    key_copy.wait()
+    chunk = 256 // page_tok
+    new = lax.broadcasted_iota(jnp.int32, (256, 256), 0)
+    old = lax.broadcasted_iota(jnp.int32, (256, 256), 1)
+    moves = (new // chunk == lax.rem(old, page_tok)) & (lax.rem(new, chunk) == old // page_tok)
+    moves = jnp.where(moves, 1.0, 0.0).astype(jnp.bfloat16)
+    for copy, source, target in (
+        (key_copy, keys, keys_by_token), (value_copy, values, values_by_token)
+    ):
+        copy.wait()
+        for c in range(0, slots, chunk):
+            moved = jnp.dot(
+                moves, source[c : c + chunk].reshape(256, source.shape[2]),
+                preferred_element_type=jnp.float32,
+            )
+            target[:, c : c + chunk, :] = moved.astype(jnp.bfloat16).reshape(
+                page_tok, chunk, source.shape[2]
+            )
+
     for k in range(1, insts):
         for copy in gather_copies(k):
             copy.wait()
@@ -151,14 +164,18 @@
                 code += jnp.where(
                     slot_id == page_id[r : r + 1, b : b + 128], page_code[r : r + 1, b : b + 128], 0
                 )
-    code = jnp.sum(code.astype(jnp.float32), axis=1, keepdims=True).astype(jnp.int32)
-    lane_request = lax.rem(lax.broadcasted_iota(jnp.int32, (slots, lanes), 1), width) // per_group
-    filled = jnp.where(lane_request == code >> 5, code & 31, 0)
-
-    offset = lax.broadcasted_iota(jnp.int32, (CHUNK_SLOTS, page_tok, lanes), 1)
-    lane = lax.broadcasted_iota(jnp.int32, (HEAD_SIZE, lanes), 1)
-    chunk_tokens = CHUNK_SLOTS * page_tok
-    chunks = [slice(c * CHUNK_SLOTS, (c + 1) * CHUNK_SLOTS) for c in range(slots // CHUNK_SLOTS)]
+    code = jnp.sum(code.astype(jnp.float32).T, axis=0, keepdims=True).astype(jnp.int32)
+    slot_owner = jnp.broadcast_to(code >> 5, (BLOCK_ROWS, slots))
+    slot_fill = jnp.broadcast_to(code & 31, (BLOCK_ROWS, slots))
+    block_row = lax.broadcasted_iota(jnp.int32, (BLOCK_ROWS, slots), 0)
+    lane = lax.broadcasted_iota(jnp.int32, (BLOCK_ROWS, 128), 1)
+
+    def tree(join, items):
+        while len(items) > 1:
+            items = [join(*items[k : k + 2]) for k in range(0, len(items) - 1, 2)] + (
+                items[-1:] if len(items) % 2 else []
+            )
+        return items[0]
 
     def exchange(to_i, to_p):
         to = to_i * pages + to_p
@@ -175,37 +192,56 @@
         pair_queries = jnp.concatenate(
             [jnp.concatenate([low, none], axis=1), jnp.concatenate([none, high], axis=1)], axis=0
         )
-        for here in chunks:
-            scores = lax.dot_general(
-                keys[here, :, cut].reshape(chunk_tokens, 2 * HEAD_SIZE),
-                pair_queries,
-                (((1,), (1,)), ((), ())),
-                preferred_element_type=jnp.float32,
-            ).reshape(CHUNK_SLOTS, page_tok, lanes)
-            masked = jnp.where(offset < filled[here][:, None, :], scores, LOWEST_SCORE)
-            top = jnp.max(masked, axis=1)
-            page_max[pair, here] = top
-            raw[pair, here] = jnp.exp2((masked - top[:, None, :]) * EXPONENT)
-        tops = page_max[pair]
-        local_max = jnp.max(tops, axis=0, keepdims=True)
-        factor = jnp.where(filled > 0, jnp.exp2((tops - local_max) * EXPONENT), 0.0)
-        total = jnp.zeros((page_tok, lanes), jnp.float32)
-        for c, here in enumerate(chunks):
-            scale = factor[here][:, None, :]
-            weight = raw[pair, here]
-            total += jnp.sum(weight * scale, axis=0)
-            scaled = weight.astype(jnp.bfloat16).astype(jnp.float32) * scale
-            upper = scaled.astype(jnp.bfloat16)
-            lower = (scaled - upper.astype(jnp.float32)).astype(jnp.bfloat16)
-            rows = slice(c * chunk_tokens, (c + 1) * chunk_tokens)
-            weights[pair, rows, :lanes] = upper.reshape(chunk_tokens, lanes)
-            weights[pair, rows, lanes:] = lower.reshape(chunk_tokens, lanes)
-        total = jnp.sum(total, axis=0, keepdims=True)
-        both = jnp.dot(values_t[pair], weights[pair], preferred_element_type=jnp.float32)
-        both = both[:, :lanes] + both[:, lanes:]
-        part = jnp.where(lane < width, both[:HEAD_SIZE], both[HEAD_SIZE:]).T
+        scores[pair] = lax.dot_general(
+            pair_queries,
+            keys_by_token[:, :, cut].reshape(tokens, 2 * HEAD_SIZE),
+            (((1,), (1,)), ((), ())),
+            preferred_element_type=jnp.float32,
+        )
+
+        def weigh(block, pair=pair):
+            first = block * BLOCK_ROWS
+            if not isinstance(block, int):
+                first = pl.multiple_of(first, BLOCK_ROWS)
+            row_request = lax.rem(first + block_row, width) // per_group
+            filled = jnp.where(slot_owner == row_request, slot_fill, 0)
+            masked = [
+                jnp.where(
+                    filled > t,
+                    scores[pair, pl.ds(first, BLOCK_ROWS), t * slots : (t + 1) * slots],
+                    LOWEST_SCORE,
+                )
+                for t in range(page_tok)
+            ]
+            page_max = tree(jnp.maximum, masked)
+            raw = [jnp.exp2((x - page_max) * EXPONENT) for x in masked]
+            page_sum = tree(jnp.add, raw)
+            local_max = jnp.max(page_max, axis=1, keepdims=True)
+            factor = jnp.where(filled > 0, jnp.exp2((page_max - local_max) * EXPONENT), 0.0)
+            total = jnp.sum(page_sum * factor, axis=1, keepdims=True)
+            for t in range(page_tok):
+                scaled = raw[t].astype(jnp.bfloat16).astype(jnp.float32) * factor
+                upper = scaled.astype(jnp.bfloat16)
+                lower = (scaled - upper.astype(jnp.float32)).astype(jnp.bfloat16)
+                at = slice(t * slots, (t + 1) * slots)
+                weights[pair, pl.ds(first, BLOCK_ROWS), at] = upper
+                weights[pair, pl.ds(lanes + first, BLOCK_ROWS), at] = lower
+            columns_of[pair, pl.ds(first, BLOCK_ROWS)] = jnp.where(lane == 0, local_max, total)
+
+        if lanes <= 128:
+            for block in range(lanes // BLOCK_ROWS):
+                weigh(block)
+        else:
+            lax.fori_loop(0, lanes // BLOCK_ROWS, lambda block, carry: (weigh(block), carry)[1], 0)
+        both = jnp.dot(
+            weights[pair], values_by_token[:, :, cut].reshape(tokens, 2 * HEAD_SIZE),
+            preferred_element_type=jnp.float32,
+        )
+        both = both[:lanes] + both[lanes:]
+        part = jnp.concatenate([both[:width, :HEAD_SIZE], both[width:, HEAD_SIZE:]], axis=0)
+        stats = columns_of[pair].T
         stats = jnp.concatenate(
-            [x[:, b * 128 : (b + 1) * 128] for x in (local_max, total) for b in range(stat_rows)],
+            [stats[k : k + 1, b * 128 : (b + 1) * 128] for k in range(2) for b in range(stat_rows)],
             axis=0,
         )
         targets = [
@@ -311,16 +347,17 @@
             pltpu.VMEM(block_table.shape, jnp.int32),
             pltpu.VMEM((slots, page_tok, depth), jnp.bfloat16),
             pltpu.VMEM((slots, page_tok, depth), jnp.bfloat16),
-            pltpu.VMEM((pairs, 2 * HEAD_SIZE, slots * page_tok), jnp.bfloat16),
+            pltpu.VMEM((page_tok, slots, depth), jnp.bfloat16),
+            pltpu.VMEM((page_tok, slots, depth), jnp.bfloat16),
             pltpu.VMEM((groups, own * per_group, HEAD_SIZE), jnp.bfloat16),
             pltpu.VMEM((insts, groups, own * per_group, HEAD_SIZE), jnp.bfloat16),
             pltpu.VMEM((own, columns), jnp.int32),
             pltpu.VMEM((insts, own, columns), jnp.int32),
-            pltpu.VMEM((pairs, slots, page_tok, lanes), jnp.float32),
-            pltpu.VMEM((pairs, slots, lanes), jnp.float32),
-            pltpu.VMEM((pairs, slots * page_tok, 2 * lanes), jnp.bfloat16),
+            pltpu.VMEM((pairs, lanes, slots * page_tok), jnp.float32),
+            pltpu.VMEM((pairs, 2 * lanes, slots * page_tok), jnp.bfloat16),
             pltpu.VMEM((devices, block_rows, 128), jnp.float32),
             pltpu.VMEM((devices, block_rows, 128), jnp.float32),
+            pltpu.VMEM((pairs, lanes, 128), jnp.float32),
             pltpu.VMEM((pages, unit_rows, HEAD_SIZE), jnp.float32),
             pltpu.VMEM((pages, unit_rows, HEAD_SIZE), jnp.float32),
             pltpu.VMEM((unit_rows, HEAD_SIZE), jnp.bfloat16),

time: 23.4 us -> 23.3 us (level)
  no operation moved by 1% of the time
where the time goes in v3:
time: 23.3 us; the launch traced here: 23 us
  Pallas kernels  21.6 us (93%)
  local copies, waits for them, and re-layouts  1.33 us (6%)
    pallas_call x1, Pallas kernels, shards(): pl.pallas_call(functools.partial(kernel, insts, pages, groups), out_shape...  21.6 us
    reshape x1, local copies, waits for them, and re-layouts, shards(): return out.reshape(own, heads * HEAD_SIZE)  1.33 us

profile of v3, /device:TPU:0, one launch (start us, length us, event | category | flops | bytes accessed | tf_op | source)
XLA Modules:
  0.0 23.0 jit_solution(11364178649970116815)
XLA Ops:
  0.0 21.6 %paged_attention.1 = bf16[4,16,128]{2,1,0:T(8,128)(2,1)} custom-call(bf16[2,4096]{1,0:T(2,128)(2,1)} %q_hbm.1, bf16[2,2,512]{2,1,0:T(2,128)(2,1)} %fresh_hbm.1, s32[2]{0:T(128)} %len_hbm.1, s32[2,384]{1,0:T(2,128)} %table_hbm.1, bf16[2,128,16,512]{3,2,1,0:T(8,128)(2,1)} %pool_hbm.1), custom_call_target="tpu_custom_call" | custom-call | flops 536870912 | bytes 4194304 | tf_op jit(solution)/shard_map/paged_attention/pallas_call | solution.py:338
  21.7 1.3 %reshape.3 = bf16[2,4096]{1,0:T(2,128)(2,1)} reshape(bf16[4,16,128]{2,1,0:T(8,128)(2,1)} %paged_attention.1) | data formatting | bytes 32768 | tf_op jit(solution)/shard_map/reshape | solution.py:379

commit v4 on v3

--- a/solution.py
+++ b/solution.py
@@ -25,7 +25,7 @@
     q_ref, fresh_ref, len_ref, table_ref,
     keys, values, keys_by_token, values_by_token, q_own, q_all, t_own, t_all,
     scores, weights, send, recv,
-    columns_of, fresh_score, fresh_value, result,
+    page_max, page_sum, factors, fresh_score, fresh_value, result,
     in_sem, pool_sem, q_send, q_recv, t_send, t_recv, x_send, x_recv, o_send, o_recv, o_own,
 ):
     own = q_ref.shape[0]
@@ -140,22 +140,28 @@
         (key_copy, keys, keys_by_token), (value_copy, values, values_by_token)
     ):
         copy.wait()
-        for c in range(0, slots, chunk):
-            moved = jnp.dot(
-                moves, source[c : c + chunk].reshape(256, source.shape[2]),
-                preferred_element_type=jnp.float32,
-            )
-            target[:, c : c + chunk, :] = moved.astype(jnp.bfloat16).reshape(
-                page_tok, chunk, source.shape[2]
-            )
+
+        def move(step, carry, source=source, target=target):
+            for half in range(2):
+                c = pl.multiple_of((2 * step + half) * chunk, chunk)
+                moved = jnp.dot(
+                    moves, source[pl.ds(c, chunk)].reshape(256, source.shape[2]),
+                    preferred_element_type=jnp.float32,
+                )
+                target[:, pl.ds(c, chunk), :] = moved.astype(jnp.bfloat16).reshape(
+                    page_tok, chunk, source.shape[2]
+                )
+            return carry
+
+        lax.fori_loop(0, slots // chunk // 2, move, 0)
 
     for k in range(1, insts):
         for copy in gather_copies(k):
             copy.wait()
 
     slot_id = lax.broadcasted_iota(jnp.int32, (slots, 128), 0) + me * slots
-    code = jnp.zeros((slots, 128), jnp.int32)
-    for i in range(insts):
+
+    def match(i, code):
         packed = t_all[i]
         page_id = packed >> 10
         page_code = packed & 1023
@@ -164,11 +170,15 @@
                 code += jnp.where(
                     slot_id == page_id[r : r + 1, b : b + 128], page_code[r : r + 1, b : b + 128], 0
                 )
+        return code
+
+    code = lax.fori_loop(0, insts, match, jnp.zeros((slots, 128), jnp.int32))
     code = jnp.sum(code.astype(jnp.float32).T, axis=0, keepdims=True).astype(jnp.int32)
+    code = jnp.where(code == 0, requests * 32, code)
     slot_owner = jnp.broadcast_to(code >> 5, (BLOCK_ROWS, slots))
     slot_fill = jnp.broadcast_to(code & 31, (BLOCK_ROWS, slots))
     block_row = lax.broadcasted_iota(jnp.int32, (BLOCK_ROWS, slots), 0)
-    lane = lax.broadcasted_iota(jnp.int32, (BLOCK_ROWS, 128), 1)
+    lane = lax.broadcasted_iota(jnp.int32, (lanes, 128), 1)
 
     def tree(join, items):
         while len(items) > 1:
@@ -199,13 +209,12 @@
             preferred_element_type=jnp.float32,
         )
 
-        def weigh(block, pair=pair):
-            first = block * BLOCK_ROWS
-            if not isinstance(block, int):
-                first = pl.multiple_of(first, BLOCK_ROWS)
+        def owned_tokens(first):
             row_request = lax.rem(first + block_row, width) // per_group
-            filled = jnp.where(slot_owner == row_request, slot_fill, 0)
-            masked = [
+            return jnp.where(slot_owner == row_request, slot_fill, 0)
+
+        def masked_scores(first, filled, pair=pair):
+            return [
                 jnp.where(
                     filled > t,
                     scores[pair, pl.ds(first, BLOCK_ROWS), t * slots : (t + 1) * slots],
@@ -213,12 +222,23 @@
                 )
                 for t in range(page_tok)
             ]
-            page_max = tree(jnp.maximum, masked)
-            raw = [jnp.exp2((x - page_max) * EXPONENT) for x in masked]
-            page_sum = tree(jnp.add, raw)
-            local_max = jnp.max(page_max, axis=1, keepdims=True)
-            factor = jnp.where(filled > 0, jnp.exp2((page_max - local_max) * EXPONENT), 0.0)
-            total = jnp.sum(page_sum * factor, axis=1, keepdims=True)
+
+        def maximum(block, carry):
+            first = pl.multiple_of(block * BLOCK_ROWS, BLOCK_ROWS)
+            page_max[pl.ds(first, BLOCK_ROWS)] = tree(
+                jnp.maximum, masked_scores(first, owned_tokens(first))
+            )
+            return carry
+
+        def weigh(block, carry, pair=pair):
+            first = pl.multiple_of(block * BLOCK_ROWS, BLOCK_ROWS)
+            filled = owned_tokens(first)
+            tops = page_max[pl.ds(first, BLOCK_ROWS)]
+            factor = factors[pl.ds(first, BLOCK_ROWS)]
+            raw = [
+                jnp.exp2((x - tops) * EXPONENT) for x in masked_scores(first, filled)
+            ]
+            page_sum[pl.ds(first, BLOCK_ROWS)] = tree(jnp.add, raw) * factor
             for t in range(page_tok):
                 scaled = raw[t].astype(jnp.bfloat16).astype(jnp.float32) * factor
                 upper = scaled.astype(jnp.bfloat16)
@@ -226,20 +246,25 @@
                 at = slice(t * slots, (t + 1) * slots)
                 weights[pair, pl.ds(first, BLOCK_ROWS), at] = upper
                 weights[pair, pl.ds(lanes + first, BLOCK_ROWS), at] = lower
-            columns_of[pair, pl.ds(first, BLOCK_ROWS)] = jnp.where(lane == 0, local_max, total)
-
-        if lanes <= 128:
-            for block in range(lanes // BLOCK_ROWS):
-                weigh(block)
-        else:
-            lax.fori_loop(0, lanes // BLOCK_ROWS, lambda block, carry: (weigh(block), carry)[1], 0)
+            return carry
+
+        blocks = lanes // BLOCK_ROWS
+        lax.fori_loop(0, blocks, maximum, 0)
+        tops = page_max[...]
+        local_max = jnp.max(tops, axis=1, keepdims=True)
+        all_rows = lax.broadcasted_iota(jnp.int32, (lanes, slots), 0)
+        owned = code >> 5 == lax.rem(all_rows, width) // per_group
+        factors[...] = jnp.where(owned, jnp.exp2((tops - local_max) * EXPONENT), 0.0)
+        lax.fori_loop(0, blocks, weigh, 0)
+        total = jnp.sum(page_sum[...], axis=1, keepdims=True)
+        columns_of = jnp.where(lane == 0, local_max, total)
         both = jnp.dot(
             weights[pair], values_by_token[:, :, cut].reshape(tokens, 2 * HEAD_SIZE),
             preferred_element_type=jnp.float32,
         )
         both = both[:lanes] + both[lanes:]
         part = jnp.concatenate([both[:width, :HEAD_SIZE], both[width:, HEAD_SIZE:]], axis=0)
-        stats = columns_of[pair].T
+        stats = columns_of.T
         stats = jnp.concatenate(
             [stats[k : k + 1, b * 128 : (b + 1) * 128] for k in range(2) for b in range(stat_rows)],
             axis=0,
@@ -357,7 +382,9 @@
             pltpu.VMEM((pairs, 2 * lanes, slots * page_tok), jnp.bfloat16),
             pltpu.VMEM((devices, block_rows, 128), jnp.float32),
             pltpu.VMEM((devices, block_rows, 128), jnp.float32),
-            pltpu.VMEM((pairs, lanes, 128), jnp.float32),
+            pltpu.VMEM((lanes, slots), jnp.float32),
+            pltpu.VMEM((lanes, slots), jnp.float32),
+            pltpu.VMEM((lanes, slots), jnp.float32),
             pltpu.VMEM((pages, unit_rows, HEAD_SIZE), jnp.float32),
             pltpu.VMEM((pages, unit_rows, HEAD_SIZE), jnp.float32),
             pltpu.VMEM((unit_rows, HEAD_SIZE), jnp.bfloat16),

time: 23.3 us -> 25 us (1.073)
  Pallas kernels: 21.6 us -> 23.3 us
    pallas_call x1, Pallas kernels: 21.6 us -> 23.3 us  [shards(): pl.pallas_call(functools.partial(kernel, insts, pages, groups), out_shape...]
where the time goes in v4:
time: 25 us; the launch traced here: 24.7 us
  Pallas kernels  23.3 us (93%)
  local copies, waits for them, and re-layouts  1.33 us (5%)
    pallas_call x1, Pallas kernels, shards(): pl.pallas_call(functools.partial(kernel, insts, pages, groups), out_shape...  23.3 us
    reshape x1, local copies, waits for them, and re-layouts, shards(): return out.reshape(own, heads * HEAD_SIZE)  1.33 us

profile of v4, /device:TPU:0, one launch (start us, length us, event | category | flops | bytes accessed | tf_op | source)
XLA Modules:
  0.0 24.7 jit_solution(2203241215434752198)
XLA Ops:
  0.0 23.3 %paged_attention.1 = bf16[4,16,128]{2,1,0:T(8,128)(2,1)} custom-call(bf16[2,4096]{1,0:T(2,128)(2,1)} %q_hbm.1, bf16[2,2,512]{2,1,0:T(2,128)(2,1)} %fresh_hbm.1, s32[2]{0:T(128)} %len_hbm.1, s32[2,384]{1,0:T(2,128)} %table_hbm.1, bf16[2,128,16,512]{3,2,1,0:T(8,128)(2,1)} %pool_hbm.1), custom_call_target="tpu_custom_call" | custom-call | flops 536870912 | bytes 4194304 | tf_op jit(solution)/shard_map/paged_attention/pallas_call | solution.py:363
  23.3 1.3 %reshape.3 = bf16[2,4096]{1,0:T(2,128)(2,1)} reshape(bf16[4,16,128]{2,1,0:T(8,128)(2,1)} %paged_attention.1) | data formatting | bytes 32768 | tf_op jit(solution)/shard_map/reshape | solution.py:406

commit v5 on v3

--- a/solution.py
+++ b/solution.py
@@ -12,6 +12,7 @@
 LOWEST_SCORE = -1e30
 EXPONENT = math.log2(math.e) / math.sqrt(HEAD_SIZE)
 BLOCK_ROWS = 16
+POOL_PIECES = 4
 MESH = pl.DeviceIdType.MESH
 
 
@@ -69,10 +70,17 @@
     ]
     for copy in small:
         copy.start()
-    value_copy = pltpu.make_async_copy(pool_hbm.at[1], values, pool_sem.at[1])
-    key_copy = pltpu.make_async_copy(pool_hbm.at[0], keys, pool_sem.at[0])
-    key_copy.start()
-    value_copy.start()
+    piece = slots // POOL_PIECES
+    pool_copies = [
+        pltpu.make_async_copy(
+            pool_hbm.at[kind, pl.ds(c * piece, piece)], target.at[pl.ds(c * piece, piece)],
+            pool_sem.at[kind, c],
+        )
+        for kind, target in enumerate((keys, values))
+        for c in range(POOL_PIECES)
+    ]
+    for copy in pool_copies:
+        copy.start()
     for copy in small:
         copy.wait()
 
@@ -136,11 +144,11 @@
     old = lax.broadcasted_iota(jnp.int32, (256, 256), 1)
     moves = (new // chunk == lax.rem(old, page_tok)) & (lax.rem(new, chunk) == old // page_tok)
     moves = jnp.where(moves, 1.0, 0.0).astype(jnp.bfloat16)
-    for copy, source, target in (
-        (key_copy, keys, keys_by_token), (value_copy, values, values_by_token)
-    ):
+    for k, copy in enumerate(pool_copies):
+        source, target = ((keys, keys_by_token), (values, values_by_token))[k // POOL_PIECES]
         copy.wait()
-        for c in range(0, slots, chunk):
+        base = k % POOL_PIECES * piece
+        for c in range(base, base + piece, chunk):
             moved = jnp.dot(
                 moves, source[c : c + chunk].reshape(256, source.shape[2]),
                 preferred_element_type=jnp.float32,
@@ -262,7 +270,11 @@
                 exchange(lax.rem(me_i + k, insts), p).start()
             return carry
 
-        lax.fori_loop(1, insts, start_exchange, 0)
+        if insts <= 4:
+            for k in range(1, insts):
+                start_exchange(k, 0)
+        else:
+            lax.fori_loop(1, insts, start_exchange, 0)
         for p in targets:
             @pl.when(me_p != p)
             def _():
@@ -361,7 +373,7 @@
             pltpu.VMEM((pages, unit_rows, HEAD_SIZE), jnp.float32),
             pltpu.VMEM((pages, unit_rows, HEAD_SIZE), jnp.float32),
             pltpu.VMEM((unit_rows, HEAD_SIZE), jnp.bfloat16),
-            dma((4,)), dma((2,)),
+            dma((4,)), dma((2, POOL_PIECES)),
             dma((insts,)), dma((insts,)), dma((insts,)), dma((insts,)),
             dma((devices,)), dma((devices,)),
             dma((pages,)), dma((pages,)), dma(()),

time: 23.3 us -> 23.3 us (level)
  no operation moved by 1% of the time
where the time goes in v5:
time: 23.3 us; the launch traced here: 23 us
  Pallas kernels  21.7 us (93%)
  local copies, waits for them, and re-layouts  1.33 us (6%)
    pallas_call x1, Pallas kernels, shards(): pl.pallas_call(functools.partial(kernel, insts, pages, groups), out_shape...  21.7 us
    reshape x1, local copies, waits for them, and re-layouts, shards(): return out.reshape(own, heads * HEAD_SIZE)  1.33 us

profile of v5, /device:TPU:0, one launch (start us, length us, event | category | flops | bytes accessed | tf_op | source)
XLA Modules:
  0.0 23.0 jit_solution(16408631080717965510)
XLA Ops:
  0.0 21.7 %paged_attention.1 = bf16[4,16,128]{2,1,0:T(8,128)(2,1)} custom-call(bf16[2,4096]{1,0:T(2,128)(2,1)} %q_hbm.1, bf16[2,2,512]{2,1,0:T(2,128)(2,1)} %fresh_hbm.1, s32[2]{0:T(128)} %len_hbm.1, s32[2,384]{1,0:T(2,128)} %table_hbm.1, bf16[2,128,16,512]{3,2,1,0:T(8,128)(2,1)} %pool_hbm.1), custom_call_target="tpu_custom_call" | custom-call | flops 536870912 | bytes 4194304 | tf_op jit(solution)/shard_map/paged_attention/pallas_call | solution.py:350
  21.7 1.3 %reshape.3 = bf16[2,4096]{1,0:T(2,128)(2,1)} reshape(bf16[4,16,128]{2,1,0:T(8,128)(2,1)} %paged_attention.1) | data formatting | bytes 32768 | tf_op jit(solution)/shard_map/reshape | solution.py:391

commit v6 on v5

--- a/solution.py
+++ b/solution.py
@@ -14,10 +14,6 @@
 BLOCK_ROWS = 16
 POOL_PIECES = 4
 MESH = pl.DeviceIdType.MESH
-
-
-def slot_of(pages, p):
-    return p + p // 2 - 2 * (p // 3) if pages == 4 else p
 
 
 def kernel(
@@ -41,26 +37,38 @@
     lanes = 2 * width
     stat_rows = lanes // 128
     devices = insts * pages
-    units = own * groups // pages
-    unit_rows = units * per_group
+    rows = own * per_group
+    middle = pages // 2 - 1
 
     me_i = lax.axis_index("inst")
     me_p = lax.axis_index("page")
     me = me_i * pages + me_p
-    me_slot = slot_of(pages, me_p)
+    finishes = (me_p == middle) | (me_p == middle + 1)
+    side = lax.rem(me_p + pages - middle, 2)
 
     barrier = pltpu.get_barrier_semaphore()
 
-    def greet(k, carry):
-        other = lax.rem(me + k, devices)
-        pl.semaphore_signal(
-            barrier, inc=1,
-            device_id={"inst": lax.div(other, pages), "page": lax.rem(other, pages)},
-            device_id_type=MESH,
-        )
-        return carry
-
-    lax.fori_loop(1, devices, greet, 0)
+    def greet(p, first):
+        def one(k, carry):
+            pl.semaphore_signal(
+                barrier, inc=1, device_id={"inst": lax.rem(me_i + k, insts), "page": p},
+                device_id_type=MESH,
+            )
+            return carry
+
+        lax.fori_loop(first, insts, one, 0)
+
+    greet(me_p, 1)
+
+    @pl.when(finishes)
+    def _():
+        for k in range(1, pages):
+            greet(lax.rem(me_p + k, pages), 0)
+
+    @pl.when(jnp.logical_not(finishes))
+    def _():
+        for j in range(2):
+            greet(middle + j, 0)
 
     small = [
         pltpu.make_async_copy(source, target, in_sem.at[k])
@@ -88,7 +96,7 @@
     fresh = fresh_ref[...].astype(jnp.float32)
     grouped = []
     for g in range(groups):
-        rows = jnp.concatenate(
+        stacked = jnp.concatenate(
             [
                 q[r : r + 1, (g * per_group + h) * HEAD_SIZE : (g * per_group + h + 1) * HEAD_SIZE]
                 for r in range(own)
@@ -96,8 +104,8 @@
             ],
             axis=0,
         )
-        grouped.append(rows)
-        q_own[g] = rows.astype(jnp.bfloat16)
+        grouped.append(stacked)
+        q_own[g] = stacked.astype(jnp.bfloat16)
     column = lax.broadcasted_iota(jnp.int32, (own, columns), 1)
     row = lax.broadcasted_iota(jnp.int32, (own, columns), 0)
     length = jnp.zeros((own, columns), jnp.int32)
@@ -108,7 +116,13 @@
         fill > 0, table_ref[...] * 1024 + (me_i * own + row) * 32 + fill, -1
     )
 
-    pl.semaphore_wait(barrier, devices - 1)
+    @pl.when(finishes)
+    def _():
+        pl.semaphore_wait(barrier, devices - 1)
+
+    @pl.when(jnp.logical_not(finishes))
+    def _():
+        pl.semaphore_wait(barrier, 3 * insts - 1)
 
     def gather_copies(k):
         to = {"inst": lax.rem(me_i + k, insts)}
@@ -129,15 +143,14 @@
     q_all[me_i] = q_own[...]
     t_all[me_i] = t_own[...]
 
-    for unit in range(own * groups):
-        r, g = unit // groups, unit % groups
-        slot, u = unit // units, unit % units
+    for g in range(groups):
         cut = slice(g * HEAD_SIZE, (g + 1) * HEAD_SIZE)
-        products = grouped[g][r * per_group : (r + 1) * per_group] * fresh[0, r : r + 1, cut]
-        score = jnp.sum(products, axis=1, keepdims=True)
-        place = slice(u * per_group, (u + 1) * per_group)
-        fresh_score[slot, place] = jnp.broadcast_to(score, (per_group, HEAD_SIZE))
-        fresh_value[slot, place] = jnp.broadcast_to(fresh[1, r : r + 1, cut], (per_group, HEAD_SIZE))
+        for r in range(own):
+            place = slice(r * per_group, (r + 1) * per_group)
+            products = grouped[g][place] * fresh[0, r : r + 1, cut]
+            score = jnp.sum(products, axis=1, keepdims=True)
+            fresh_score[g, place] = jnp.broadcast_to(score, (per_group, HEAD_SIZE))
+            fresh_value[g, place] = jnp.broadcast_to(fresh[1, r : r + 1, cut], (per_group, HEAD_SIZE))
 
     chunk = 256 // page_tok
     new = lax.broadcasted_iota(jnp.int32, (256, 256), 0)
@@ -185,12 +198,28 @@
             )
         return items[0]
 
-    def exchange(to_i, to_p):
-        to = to_i * pages + to_p
+    def exchange(pair, j, to_i):
         return pltpu.make_async_remote_copy(
-            src_ref=send.at[to], dst_ref=recv.at[me], send_sem=x_send.at[to],
-            recv_sem=x_recv.at[me], device_id={"inst": to_i, "page": to_p}, device_id_type=MESH,
-        )
+            src_ref=send.at[pair, j, to_i], dst_ref=recv.at[pair, me],
+            send_sem=x_send.at[pair, j, to_i], recv_sem=x_recv.at[pair, me],
+            device_id={"inst": to_i, "page": middle + j}, device_id_type=MESH,
+        )
+
+    def all_exchanges(pair, act):
+        def one(k, carry):
+            for j in range(2):
+                act(exchange(pair, j, lax.rem(me_i + k, insts)))
+            return carry
+
+        if insts <= 4:
+            for k in range(1, insts):
+                one(k, 0)
+        else:
+            lax.fori_loop(1, insts, one, 0)
+        for j in range(2):
+            @pl.when(me_p != middle + j)
+            def _():
+                act(exchange(pair, j, me_i))
 
     for pair in range(pairs):
         cut = slice(pair * 2 * HEAD_SIZE, (pair + 1) * 2 * HEAD_SIZE)
@@ -206,6 +235,9 @@
             (((1,), (1,)), ((), ())),
             preferred_element_type=jnp.float32,
         )
+
+    for pair in range(pairs):
+        cut = slice(pair * 2 * HEAD_SIZE, (pair + 1) * 2 * HEAD_SIZE)
 
         def weigh(block, pair=pair):
             first = block * BLOCK_ROWS
@@ -252,85 +284,98 @@
             [stats[k : k + 1, b * 128 : (b + 1) * 128] for k in range(2) for b in range(stat_rows)],
             axis=0,
         )
-        targets = [
-            p for p in range(pages) if slot_of(pages, p) * units % groups // 2 == pair
-        ]
-        for p in targets:
-            for i in range(insts):
-                send[i * pages + p, unit_rows:] = stats
-                for u in range(units):
-                    r, g = divmod(slot_of(pages, p) * units + u, groups)
-                    start = (g % 2) * width + (i * own + r) * per_group
-                    send[i * pages + p, u * per_group : (u + 1) * per_group] = part[
-                        start : start + per_group
-                    ]
-
-        def start_exchange(k, carry):
-            for p in targets:
-                exchange(lax.rem(me_i + k, insts), p).start()
-            return carry
-
-        if insts <= 4:
-            for k in range(1, insts):
-                start_exchange(k, 0)
-        else:
-            lax.fori_loop(1, insts, start_exchange, 0)
-        for p in targets:
-            @pl.when(me_p != p)
+        for i in range(insts):
+            for j in range(2):
+                start = j * width + i * rows
+                send[pair, j, i, :rows] = part[start : start + rows]
+                send[pair, j, i, rows:] = stats
+        all_exchanges(pair, lambda copy: copy.start())
+
+    def result_copy(pair, k):
+        at = pl.ds(pl.multiple_of((2 * pair + side) * per_group * HEAD_SIZE, 128), per_group * HEAD_SIZE)
+        return pltpu.make_async_remote_copy(
+            src_ref=result.at[pair], dst_ref=out_hbm.at[:, at], send_sem=o_send.at[pair, k],
+            recv_sem=o_recv.at[pair, side], device_id={"page": lax.rem(me_p + k, pages)},
+            device_id_type=MESH,
+        )
+
+    def own_copy(pair):
+        at = pl.ds(pl.multiple_of((2 * pair + side) * per_group * HEAD_SIZE, 128), per_group * HEAD_SIZE)
+        return pltpu.make_async_copy(result.at[pair], out_hbm.at[:, at], o_own.at[pair])
+
+    @pl.when(finishes)
+    def _():
+        row = lax.broadcasted_iota(jnp.int32, (1, rows, 128), 1)
+        lane = lax.broadcasted_iota(jnp.int32, (1, rows, 128), 2)
+        place = side * width + me_i * rows + row
+        for pair in range(pairs):
+            recv[pair, me] = send[pair, side, me_i]
+
+            def wait_exchange(k, carry, pair=pair):
+                other = lax.rem(me + k, devices)
+                pltpu.make_async_remote_copy(
+                    src_ref=send.at[pair, 0, 0], dst_ref=recv.at[pair, other],
+                    send_sem=x_send.at[pair, 0, 0], recv_sem=x_recv.at[pair, other],
+                    device_id={"inst": lax.div(other, pages), "page": lax.rem(other, pages)},
+                    device_id_type=MESH,
+                ).wait_recv()
+                return carry
+
+            lax.fori_loop(1, devices, wait_exchange, 0)
+            picked = []
+            for kind in range(2):
+                found = jnp.zeros((devices, rows, 128), jnp.float32)
+                for b in range(stat_rows):
+                    at = rows + kind * stat_rows + b
+                    found = jnp.where(place == b * 128 + lane, recv[pair, :, at : at + 1, :], found)
+                picked.append(jnp.sum(found, axis=2, keepdims=True))
+            maxima, totals = picked
+            own_score = fresh_score[2 * pair + side]
+            top = jnp.maximum(jnp.max(maxima, axis=0), own_score)
+            carried = jnp.exp2((maxima - top[None]) * EXPONENT)
+            own_weight = jnp.exp2((own_score - top) * EXPONENT)
+            denominator = own_weight + jnp.sum(carried * totals, axis=0)
+            numerator = own_weight * fresh_value[2 * pair + side] + jnp.sum(
+                carried * recv[pair, :, :rows, :], axis=0
+            )
+            attn = numerator / denominator
+            attn = jnp.concatenate(
+                [
+                    jnp.concatenate(
+                        [attn[r * per_group + h : r * per_group + h + 1] for h in range(per_group)],
+                        axis=1,
+                    )
+                    for r in range(own)
+                ],
+                axis=0,
+            )
+            result[pair] = attn.astype(result.dtype)
+            for k in range(1, pages):
+                result_copy(pair, k).start()
+            own_copy(pair).start()
+
+    for pair in range(pairs):
+        for j in range(2):
+            @pl.when(me_p != middle + j)
             def _():
-                exchange(me_i, p).start()
-
-    recv[me] = send[me]
-
-    def wait_exchange(k, carry):
-        other = lax.rem(me + k, devices)
-        pltpu.make_async_remote_copy(
-            src_ref=send.at[other], dst_ref=recv.at[other], send_sem=x_send.at[other],
-            recv_sem=x_recv.at[other],
-            device_id={"inst": lax.div(other, pages), "page": lax.rem(other, pages)},
-            device_id_type=MESH,
-        ).wait()
-        return carry
-
-    lax.fori_loop(1, devices, wait_exchange, 0)
-
-    row = lax.broadcasted_iota(jnp.int32, (1, unit_rows, 128), 1)
-    lane = lax.broadcasted_iota(jnp.int32, (1, unit_rows, 128), 2)
-    unit = me_slot * units + row // per_group
-    r, g = unit // groups, lax.rem(unit, groups)
-    place = lax.rem(g, 2) * width + (me_i * own + r) * per_group + lax.rem(row, per_group)
-    picked = []
-    for kind in range(2):
-        found = jnp.zeros((devices, unit_rows, 128), jnp.float32)
-        for b in range(stat_rows):
-            at = unit_rows + kind * stat_rows + b
-            found = jnp.where(place == b * 128 + lane, recv[:, at : at + 1, :], found)
-        picked.append(jnp.sum(found, axis=2, keepdims=True))
-    maxima, totals = picked
-    own_score = fresh_score[me_slot]
-    top = jnp.maximum(jnp.max(maxima, axis=0), own_score)
-    carried = jnp.exp2((maxima - top[None]) * EXPONENT)
-    own_weight = jnp.exp2((own_score - top) * EXPONENT)
-    denominator = own_weight + jnp.sum(carried * totals, axis=0)
-    numerator = own_weight * fresh_value[me_slot] + jnp.sum(
-        carried * recv[:, :unit_rows, :], axis=0
-    )
-    result[...] = (numerator / denominator).astype(result.dtype)
-
-    def result_copy(k):
-        return pltpu.make_async_remote_copy(
-            src_ref=result, dst_ref=out_hbm.at[me_slot], send_sem=o_send.at[k],
-            recv_sem=o_recv.at[k], device_id={"page": lax.rem(me_p + k, pages)},
-            device_id_type=MESH,
-        )
-
-    for k in range(1, pages):
-        result_copy(k).start()
-    own_copy = pltpu.make_async_copy(result, out_hbm.at[me_slot], o_own)
-    own_copy.start()
-    own_copy.wait()
-    for k in range(1, pages):
-        result_copy(k).wait()
+                at = slice(
+                    (2 * pair + j) * per_group * HEAD_SIZE, (2 * pair + j + 1) * per_group * HEAD_SIZE
+                )
+                pltpu.make_async_remote_copy(
+                    src_ref=result.at[pair], dst_ref=out_hbm.at[:, at], send_sem=o_send.at[pair, 0],
+                    recv_sem=o_recv.at[pair, j], device_id={"page": middle + j},
+                    device_id_type=MESH,
+                ).wait_recv()
+
+    @pl.when(finishes)
+    def _():
+        for pair in range(pairs):
+            own_copy(pair).wait()
+            for k in range(1, pages):
+                result_copy(pair, k).wait_send()
+
+    for pair in range(pairs):
+        all_exchanges(pair, lambda copy: copy.wait_send())
 
 
 def shards(insts, pages, queries, fresh_key_value, key_value_pool, block_table, lengths):
@@ -343,13 +388,13 @@
     columns = block_table.shape[1]
     lanes = 2 * own * insts * per_group
     devices = insts * pages
-    unit_rows = own * heads // pages
-    block_rows = unit_rows + 2 * lanes // 128
+    rows = own * per_group
+    block_rows = rows + 2 * lanes // 128
     hbm = pl.BlockSpec(memory_space=pl.ANY)
     dma = pltpu.SemaphoreType.DMA
-    out = pl.pallas_call(
+    return pl.pallas_call(
         functools.partial(kernel, insts, pages, groups),
-        out_shape=jax.ShapeDtypeStruct((pages, unit_rows, HEAD_SIZE), jnp.bfloat16),
+        out_shape=jax.ShapeDtypeStruct(queries.shape, jnp.bfloat16),
         in_specs=[hbm] * 5,
         out_specs=hbm,
         scratch_shapes=[
@@ -367,16 +412,16 @@
             pltpu.VMEM((insts, own, columns), jnp.int32),
             pltpu.VMEM((pairs, lanes, slots * page_tok), jnp.float32),
             pltpu.VMEM((pairs, 2 * lanes, slots * page_tok), jnp.bfloat16),
-            pltpu.VMEM((devices, block_rows, 128), jnp.float32),
-            pltpu.VMEM((devices, block_rows, 128), jnp.float32),
+            pltpu.VMEM((pairs, 2, insts, block_rows, 128), jnp.float32),
+            pltpu.VMEM((pairs, devices, block_rows, 128), jnp.float32),
             pltpu.VMEM((pairs, lanes, 128), jnp.float32),
-            pltpu.VMEM((pages, unit_rows, HEAD_SIZE), jnp.float32),
-            pltpu.VMEM((pages, unit_rows, HEAD_SIZE), jnp.float32),
-            pltpu.VMEM((unit_rows, HEAD_SIZE), jnp.bfloat16),
+            pltpu.VMEM((groups, rows, HEAD_SIZE), jnp.float32),
+            pltpu.VMEM((groups, rows, HEAD_SIZE), jnp.float32),
+            pltpu.VMEM((pairs, own, per_group * HEAD_SIZE), jnp.bfloat16),
             dma((4,)), dma((2, POOL_PIECES)),
             dma((insts,)), dma((insts,)), dma((insts,)), dma((insts,)),
-            dma((devices,)), dma((devices,)),
-            dma((pages,)), dma((pages,)), dma(()),
+            dma((pairs, 2, insts)), dma((pairs, devices)),
+            dma((pairs, pages)), dma((pairs, 2)), dma((pairs,)),
         ],
         compiler_params=pltpu.CompilerParams(
             collective_id=0, has_side_effects=True, vmem_limit_bytes=56 * 1024 * 1024
@@ -388,7 +433,6 @@
         ),
         name="paged_attention",
     )(queries, fresh_key_value, lengths, block_table, key_value_pool)
-    return out.reshape(own, heads * HEAD_SIZE)
 
 
 def solution(mesh):

time: 23.3 us -> 22.1 us (0.948)
  Pallas kernels: 21.7 us -> 20.5 us
    unnamed x0 -> x1, local copies, waits for them, and re-layouts: none -> 1.34 us
    reshape x1 -> x0, local copies, waits for them, and re-layouts: 1.33 us -> none  [shards(): return out.reshape(own, heads * HEAD_SIZE)]
    pallas_call x1, Pallas kernels: 21.7 us -> 20.5 us  [shards(): pl.pallas_call(functools.partial(kernel, insts, pages, groups), out_shape...]
where the time goes in v6:
time: 22.1 us; the launch traced here: 21.9 us
  Pallas kernels  20.5 us (93%)
  local copies, waits for them, and re-layouts  1.34 us (6%)
    pallas_call x1, Pallas kernels, shards(): pl.pallas_call(functools.partial(kernel, insts, pages, groups), out_shape...  20.5 us
    unnamed x1, local copies, waits for them, and re-layouts  1.34 us

profile of v6, /device:TPU:0, one launch (start us, length us, event | category | flops | bytes accessed | tf_op | source)
XLA Modules:
  0.0 21.9 jit_solution(14889972193813735632)
XLA Ops:
  0.0 20.5 %paged_attention.1 = bf16[2,4096]{1,0:T(2,128)(2,1)} custom-call(bf16[2,4096]{1,0:T(2,128)(2,1)} %q_hbm.1, bf16[2,2,512]{2,1,0:T(2,128)(2,1)} %fresh_hbm.1, s32[2]{0:T(128)} %len_hbm.1, s32[2,384]{1,0:T(2,128)} %table_hbm.1, bf16[2,128,16,512]{3,2,1,0:T(8,128)(2,1)} %pool_hbm.1), custom_call_target="tpu_custom_call" | custom-call | flops 536870912 | bytes 4194304 | tf_op jit(solution)/shard_map/paged_attention/pallas_call | solution.py:395
  20.5 1.3 %copy.7 = bf16[2,4096]{1,0:T(2,128)(2,1)} copy(bf16[2,4096]{1,0:T(2,128)(2,1)} %paged_attention.1) | data formatting | bytes 32768

commit v7 on v6

--- a/solution.py
+++ b/solution.py
@@ -244,10 +244,10 @@
             if not isinstance(block, int):
                 first = pl.multiple_of(first, BLOCK_ROWS)
             row_request = lax.rem(first + block_row, width) // per_group
-            filled = jnp.where(slot_owner == row_request, slot_fill, 0)
+            owned = (slot_owner == row_request) & (slot_fill > 0)
             masked = [
                 jnp.where(
-                    filled > t,
+                    slot_fill > t,
                     scores[pair, pl.ds(first, BLOCK_ROWS), t * slots : (t + 1) * slots],
                     LOWEST_SCORE,
                 )
@@ -256,8 +256,10 @@
             page_max = tree(jnp.maximum, masked)
             raw = [jnp.exp2((x - page_max) * EXPONENT) for x in masked]
             page_sum = tree(jnp.add, raw)
-            local_max = jnp.max(page_max, axis=1, keepdims=True)
-            factor = jnp.where(filled > 0, jnp.exp2((page_max - local_max) * EXPONENT), 0.0)
+            local_max = jnp.max(
+                jnp.where(owned, page_max, LOWEST_SCORE), axis=1, keepdims=True
+            )
+            factor = jnp.where(owned, jnp.exp2((page_max - local_max) * EXPONENT), 0.0)
             total = jnp.sum(page_sum * factor, axis=1, keepdims=True)
             for t in range(page_tok):
                 scaled = raw[t].astype(jnp.bfloat16).astype(jnp.float32) * factor
@@ -378,6 +380,12 @@
         all_exchanges(pair, lambda copy: copy.wait_send())
 
 
+def settle(source, target, sem):
+    copy = pltpu.make_async_copy(source, target, sem)
+    copy.start()
+    copy.wait()
+
+
 def shards(insts, pages, queries, fresh_key_value, key_value_pool, block_table, lengths):
     own = queries.shape[0]
     slots, page_tok, depth = key_value_pool.shape[1:]
@@ -392,7 +400,7 @@
     block_rows = rows + 2 * lanes // 128
     hbm = pl.BlockSpec(memory_space=pl.ANY)
     dma = pltpu.SemaphoreType.DMA
-    return pl.pallas_call(
+    out = pl.pallas_call(
         functools.partial(kernel, insts, pages, groups),
         out_shape=jax.ShapeDtypeStruct(queries.shape, jnp.bfloat16),
         in_specs=[hbm] * 5,
@@ -433,6 +441,15 @@
         ),
         name="paged_attention",
     )(queries, fresh_key_value, lengths, block_table, key_value_pool)
+    return pl.pallas_call(
+        settle,
+        out_shape=jax.ShapeDtypeStruct(out.shape, out.dtype),
+        in_specs=[hbm],
+        out_specs=hbm,
+        scratch_shapes=[dma(())],
+        compiler_params=pltpu.CompilerParams(vmem_limit_bytes=56 * 1024 * 1024),
+        name="settle",
+    )(out)
 
 
 def solution(mesh):

time: 22.1 us -> 22.3 us (level)
  Pallas kernels: 20.5 us -> 22.1 us
  local copies, waits for them, and re-layouts: 1.34 us -> 0 us
    pallas_call x0 -> x1, Pallas kernels: none -> 1.61 us  [shards(): pl.pallas_call(settle, out_shape=jax.ShapeDtypeStruct(out.shape, out.dtyp...]
    unnamed x1 -> x0, local copies, waits for them, and re-layouts: 1.34 us -> none
where the time goes in v7:
time: 22.3 us; the launch traced here: 22.1 us
  Pallas kernels  22.1 us (99%)
    pallas_call x1, Pallas kernels, shards(): pl.pallas_call(functools.partial(kernel, insts, pages, groups), out_shape...  20.5 us
    pallas_call x1, Pallas kernels, shards(): pl.pallas_call(settle, out_shape=jax.ShapeDtypeStruct(out.shape, out.dtyp...  1.61 us

profile of v7, /device:TPU:0, one launch (start us, length us, event | category | flops | bytes accessed | tf_op | source)
XLA Modules:
  0.0 22.1 jit_solution(16630506250914251593)
XLA Ops:
  0.0 20.5 %paged_attention.1.source = bf16[2,4096]{1,0:T(2,128)(2,1)} custom-call(bf16[2,4096]{1,0:T(2,128)(2,1)} %q_hbm.1, bf16[2,2,512]{2,1,0:T(2,128)(2,1)} %fresh_hbm.1, s32[2]{0:T(128)} %len_hbm.1, s32[2,384]{1,0:T(2,128)} %table_hbm.1, bf16[2,128,16,512]{3,2,1,0:T(8,128)(2,1)} %pool_hbm.1), custom_call_target="tpu_custom_call" | custom-call | flops 536870912 | bytes 4194304 | tf_op jit(solution)/shard_map/paged_attention/pallas_call | solution.py:403
  20.5 1.6 %settle.1 = bf16[2,4096]{1,0:T(2,128)(2,1)} custom-call(bf16[2,4096]{1,0:T(2,128)(2,1)} %paged_attention.1.source), custom_call_target="tpu_custom_call" | custom-call | tf_op jit(solution)/shard_map/settle/pallas_call | solution.py:444

commit v8 on v6

--- a/solution.py
+++ b/solution.py
@@ -20,7 +20,7 @@
     insts, pages, groups,
     q_hbm, fresh_hbm, len_hbm, table_hbm, pool_hbm, out_hbm,
     q_ref, fresh_ref, len_ref, table_ref,
-    keys, values, keys_by_token, values_by_token, q_own, q_all, t_own, t_all,
+    keys, values, keys_by_token, values_by_token, keys_t, q_own, q_all, t_own, t_all,
     scores, weights, send, recv,
     columns_of, fresh_score, fresh_value, result,
     in_sem, pool_sem, q_send, q_recv, t_send, t_recv, x_send, x_recv, o_send, o_recv, o_own,
@@ -160,6 +160,9 @@
     for k, copy in enumerate(pool_copies):
         source, target = ((keys, keys_by_token), (values, values_by_token))[k // POOL_PIECES]
         copy.wait()
+        if k == POOL_PIECES:
+            for t in range(page_tok):
+                keys_t[:, t * slots : (t + 1) * slots] = keys_by_token[t].T
         base = k % POOL_PIECES * piece
         for c in range(base, base + piece, chunk):
             moved = jnp.dot(
@@ -231,8 +234,8 @@
         )
         scores[pair] = lax.dot_general(
             pair_queries,
-            keys_by_token[:, :, cut].reshape(tokens, 2 * HEAD_SIZE),
-            (((1,), (1,)), ((), ())),
+            keys_t[cut],
+            (((1,), (0,)), ((), ())),
             preferred_element_type=jnp.float32,
         )
 
@@ -244,10 +247,10 @@
             if not isinstance(block, int):
                 first = pl.multiple_of(first, BLOCK_ROWS)
             row_request = lax.rem(first + block_row, width) // per_group
-            filled = jnp.where(slot_owner == row_request, slot_fill, 0)
+            owned = (slot_owner == row_request) & (slot_fill > 0)
             masked = [
                 jnp.where(
-                    filled > t,
+                    slot_fill > t,
                     scores[pair, pl.ds(first, BLOCK_ROWS), t * slots : (t + 1) * slots],
                     LOWEST_SCORE,
                 )
@@ -256,8 +259,10 @@
             page_max = tree(jnp.maximum, masked)
             raw = [jnp.exp2((x - page_max) * EXPONENT) for x in masked]
             page_sum = tree(jnp.add, raw)
-            local_max = jnp.max(page_max, axis=1, keepdims=True)
-            factor = jnp.where(filled > 0, jnp.exp2((page_max - local_max) * EXPONENT), 0.0)
+            local_max = jnp.max(
+                jnp.where(owned, page_max, LOWEST_SCORE), axis=1, keepdims=True
+            )
+            factor = jnp.where(owned, jnp.exp2((page_max - local_max) * EXPONENT), 0.0)
             total = jnp.sum(page_sum * factor, axis=1, keepdims=True)
             for t in range(page_tok):
                 scaled = raw[t].astype(jnp.bfloat16).astype(jnp.float32) * factor
@@ -406,6 +411,7 @@
             pltpu.VMEM((slots, page_tok, depth), jnp.bfloat16),
             pltpu.VMEM((page_tok, slots, depth), jnp.bfloat16),
             pltpu.VMEM((page_tok, slots, depth), jnp.bfloat16),
+            pltpu.VMEM((depth, slots * page_tok), jnp.bfloat16),
             pltpu.VMEM((groups, own * per_group, HEAD_SIZE), jnp.bfloat16),
             pltpu.VMEM((insts, groups, own * per_group, HEAD_SIZE), jnp.bfloat16),
             pltpu.VMEM((own, columns), jnp.int32),

time: 22.1 us -> 22 us (level)
  no operation moved by 1% of the time
where the time goes in v8:
time: 22 us; the launch traced here: 21.7 us
  Pallas kernels  20.4 us (93%)
  local copies, waits for them, and re-layouts  1.34 us (6%)
    pallas_call x1, Pallas kernels, shards(): pl.pallas_call(functools.partial(kernel, insts, pages, groups), out_shape...  20.4 us
    unnamed x1, local copies, waits for them, and re-layouts  1.34 us

profile of v8, /device:TPU:0, one launch (start us, length us, event | category | flops | bytes accessed | tf_op | source)
XLA Modules:
  0.0 21.7 jit_solution(17028580915418516428)
XLA Ops:
  0.0 20.4 %paged_attention.1 = bf16[2,4096]{1,0:T(2,128)(2,1)} custom-call(bf16[2,4096]{1,0:T(2,128)(2,1)} %q_hbm.1, bf16[2,2,512]{2,1,0:T(2,128)(2,1)} %fresh_hbm.1, s32[2]{0:T(128)} %len_hbm.1, s32[2,384]{1,0:T(2,128)} %table_hbm.1, bf16[2,128,16,512]{3,2,1,0:T(8,128)(2,1)} %pool_hbm.1), custom_call_target="tpu_custom_call" | custom-call | flops 536870912 | bytes 4194304 | tf_op jit(solution)/shard_map/paged_attention/pallas_call | solution.py:400
  20.4 1.3 %copy.7 = bf16[2,4096]{1,0:T(2,128)(2,1)} copy(bf16[2,4096]{1,0:T(2,128)(2,1)} %paged_attention.1) | data formatting | bytes 32768

commit v9 on v8

--- a/solution.py
+++ b/solution.py
@@ -20,7 +20,7 @@
     insts, pages, groups,
     q_hbm, fresh_hbm, len_hbm, table_hbm, pool_hbm, out_hbm,
     q_ref, fresh_ref, len_ref, table_ref,
-    keys, values, keys_by_token, values_by_token, keys_t, q_own, q_all, t_own, t_all,
+    keys, values, keys_by_token, values_by_token, q_own, q_all, t_own, t_all,
     scores, weights, send, recv,
     columns_of, fresh_score, fresh_value, result,
     in_sem, pool_sem, q_send, q_recv, t_send, t_recv, x_send, x_recv, o_send, o_recv, o_own,
@@ -160,9 +160,6 @@
     for k, copy in enumerate(pool_copies):
         source, target = ((keys, keys_by_token), (values, values_by_token))[k // POOL_PIECES]
         copy.wait()
-        if k == POOL_PIECES:
-            for t in range(page_tok):
-                keys_t[:, t * slots : (t + 1) * slots] = keys_by_token[t].T
         base = k % POOL_PIECES * piece
         for c in range(base, base + piece, chunk):
             moved = jnp.dot(
@@ -234,8 +231,8 @@
         )
         scores[pair] = lax.dot_general(
             pair_queries,
-            keys_t[cut],
-            (((1,), (0,)), ((), ())),
+            keys_by_token[:, :, cut].reshape(tokens, 2 * HEAD_SIZE),
+            (((1,), (1,)), ((), ())),
             preferred_element_type=jnp.float32,
         )
 
@@ -411,7 +408,6 @@
             pltpu.VMEM((slots, page_tok, depth), jnp.bfloat16),
             pltpu.VMEM((page_tok, slots, depth), jnp.bfloat16),
             pltpu.VMEM((page_tok, slots, depth), jnp.bfloat16),
-            pltpu.VMEM((depth, slots * page_tok), jnp.bfloat16),
             pltpu.VMEM((groups, own * per_group, HEAD_SIZE), jnp.bfloat16),
             pltpu.VMEM((insts, groups, own * per_group, HEAD_SIZE), jnp.bfloat16),
             pltpu.VMEM((own, columns), jnp.int32),

time: 22 us -> 22.1 us (level)
  no operation moved by 1% of the time
where the time goes in v9:
time: 22.1 us; the launch traced here: 21.9 us
  Pallas kernels  20.5 us (93%)
  local copies, waits for them, and re-layouts  1.34 us (6%)
    pallas_call x1, Pallas kernels, shards(): pl.pallas_call(functools.partial(kernel, insts, pages, groups), out_shape...  20.5 us
    unnamed x1, local copies, waits for them, and re-layouts  1.34 us

profile of v9, /device:TPU:0, one launch (start us, length us, event | category | flops | bytes accessed | tf_op | source)
XLA Modules:
  0.0 21.9 jit_solution(9909259772209705762)
XLA Ops:
  0.0 20.5 %paged_attention.1 = bf16[2,4096]{1,0:T(2,128)(2,1)} custom-call(bf16[2,4096]{1,0:T(2,128)(2,1)} %q_hbm.1, bf16[2,2,512]{2,1,0:T(2,128)(2,1)} %fresh_hbm.1, s32[2]{0:T(128)} %len_hbm.1, s32[2,384]{1,0:T(2,128)} %table_hbm.1, bf16[2,128,16,512]{3,2,1,0:T(8,128)(2,1)} %pool_hbm.1), custom_call_target="tpu_custom_call" | custom-call | flops 536870912 | bytes 4194304 | tf_op jit(solution)/shard_map/paged_attention/pallas_call | solution.py:397
  20.5 1.3 %copy.7 = bf16[2,4096]{1,0:T(2,128)(2,1)} copy(bf16[2,4096]{1,0:T(2,128)(2,1)} %paged_attention.1) | data formatting | bytes 32768
